TPU v7x, 512 devices: a whole 4x4x16 slice. The times are simulated.
512 devices in a mesh: mem: 16 (over z_lo, core), lat: 32 (over z_hi, x, y).
Axes of the slice: x: 4, y: 4, z: 16 (z_hi: 2, z_lo: 8; z = z_hi * 8 + z_lo), core: 2. Of those that a mesh axis runs over, the one named last changes fastest.
Arguments:
- ensemble: float32 [1024, 256, 512], P('mem', 'lat'), may hold values from -6 to 6
- diffusivity: float32 [256, 512], P('lat'), may hold values from 0.02 to 0.2
- north_wind: float32 [256, 512], P('lat'), may hold values from -0.25 to 0.25
- observed_blocks: int32 [32, 16, 4], P('lat'), may hold values from 0 to 31
- eastern_average_flags: int32 [32, 16, 512], P('lat'), may hold values 0 or 1
- observed_values: float32 [32, 16, 512], P('lat', 'mem'), may hold values from -6 to 6
- observed_error: float32 [32, 16, 512], P('lat', 'mem'), may hold values from 0.5 to 4
Outputs:
- analysis: float32 [1024, 256, 512], P('mem', 'lat')
Inputs may be any that keep to these rules, and one draw needn't show every extreme that they name: `observed_blocks`: block i covers a band's flattened cells i * 128 to (i + 1) * 128 - 1; blocks may repeat.
All inputs are finite; a program needn't handle non-finite values. No bound on the sum of `eastern_average_flags` on one device may be relied on, other than what follows from the above.
Results may differ from a plain program's by a relative error of at most 0.0003.
Values sent between devices are 32-bit elements; how exact they have to be, the bound alone decides.
A program may use at most 64 MiB of HBM per device.

v0:
```python
import jax
import jax.numpy as jnp
from jax import lax
from jax.sharding import PartitionSpec as P

OBS = 512
BLOCK = 128
NEWTON = 4


ADVECTION = 0.1
HIGHEST = lax.Precision.HIGHEST


def with_halo(block, sides, width):
    for axis, dim in sides:
        count = lax.axis_size(axis)
        forward = [(i, i + 1) for i in range(count - 1)]
        backward = [(target, source) for source, target in forward]
        low = lax.ppermute(
            lax.slice_in_dim(block, block.shape[dim] - width, None, axis=dim), axis, forward
        )
        high = lax.ppermute(lax.slice_in_dim(block, 0, width, axis=dim), axis, backward)
        block = jnp.concatenate([low, block, high], axis=dim)
    return block


def advance(padded, diffusivity, north_wind):
    centre = padded[:, 1:-1, :]
    northern = padded[:, :-2, :]
    equatorward_side = padded[:, 2:, :]
    eastern = jnp.roll(centre, -1, axis=2)
    western_neighbour = jnp.roll(centre, 1, axis=2)
    return (
        centre
        - ADVECTION * centre * (eastern - western_neighbour)
        - north_wind * (equatorward_side - northern)
        + diffusivity * (eastern + western_neighbour + northern + equatorward_side - 4.0 * centre)
    )


def contract_first(left, right):
    return lax.dot_general(
        left, right, (((0,), (0,)), ((), ())), precision=HIGHEST, preferred_element_type=jnp.float32
    )


def patch_gain(cell_values, seen_values, values, errors):
    sample_states = cell_values.shape[0]
    cell_offset = cell_values - jnp.mean(cell_values, axis=0)
    seen_mean = jnp.mean(seen_values, axis=0)
    seen_offset = seen_values - seen_mean
    covariance = contract_first(seen_offset, seen_offset) / (sample_states - 1.0) + jnp.diag(errors)
    row_scale = jnp.sum(jnp.abs(covariance), axis=1)
    inverse = jnp.diag(1.0 / row_scale)
    for sweep in range(NEWTON):
        product = jnp.dot(
            covariance, inverse, precision=HIGHEST, preferred_element_type=jnp.float32
        )
        inverse = 2.0 * inverse - jnp.dot(
            inverse, product, precision=HIGHEST, preferred_element_type=jnp.float32
        )
    cross_cov = contract_first(cell_offset, seen_offset) / (sample_states - 1.0)
    gain = jnp.dot(cross_cov, inverse, precision=HIGHEST, preferred_element_type=jnp.float32)
    innovation = values - seen_mean
    return (gain, innovation, seen_mean)


def body(
    ensemble,
    diffusivity,
    north_wind,
    observed_blocks,
    eastern_average_flags,
    observed_values,
    observed_error,
):
    local_members, row_count, meridian_total = ensemble.shape
    patch_count = lax.axis_size("mem")
    cell_count = row_count * meridian_total // patch_count
    variable_layers = ensemble
    for sweep in range(2):
        padded = with_halo(variable_layers, (("lat", 1),), 1)
        variable_layers = advance(padded, diffusivity, north_wind)
    block_tiles = variable_layers.reshape(local_members, row_count * meridian_total // BLOCK, BLOCK)
    east_tiles = jnp.roll(variable_layers, -1, axis=2).reshape(
        local_members, row_count * meridian_total // BLOCK, BLOCK
    )
    chosen = observed_blocks[0].reshape(-1)
    direct = jnp.take(block_tiles, chosen, axis=1).reshape(local_members, patch_count, OBS)
    shifted = jnp.take(east_tiles, chosen, axis=1).reshape(local_members, patch_count, OBS)
    observed = jnp.where(eastern_average_flags[0][None] == 1, 0.5 * (direct + shifted), direct)
    owned = variable_layers.reshape(local_members, patch_count, cell_count)
    cell_values, seen_values = (
        lax.all_to_all(owned, "mem", split_axis=1, concat_axis=0, tiled=True),
        lax.all_to_all(observed, "mem", split_axis=1, concat_axis=0, tiled=True),
    )
    cell_values = cell_values[:, 0, :]
    seen_values = seen_values[:, 0, :]
    gain, innovation, seen_mean = patch_gain(
        cell_values, seen_values, observed_values[0, 0], observed_error[0, 0]
    )
    weights = innovation[None, :] - 0.5 * (seen_values - seen_mean[None, :])
    update = lax.dot_general(
        weights,
        gain,
        (((1,), (1,)), ((), ())),
        precision=HIGHEST,
        preferred_element_type=jnp.float32,
    )
    analysed = (cell_values + update)[:, None, :]
    returned = lax.all_to_all(analysed, "mem", split_axis=0, concat_axis=1, tiled=True)
    return returned.reshape(local_members, row_count, meridian_total)


def solution(mesh):
    return jax.shard_map(
        body,
        mesh=mesh,
        in_specs=(
            P("mem", "lat", None),
            P("lat", None),
            P("lat", None),
            P("lat", None, None),
            P("lat", None, None),
            P("lat", "mem", None),
            P("lat", "mem", None),
        ),
        out_specs=P("mem", "lat", None),
        check_vma=False,
    )
```

profile of v0, /device:TPU:481, one launch (start us, length us, event | category | flops | bytes accessed | tf_op | source)
XLA Modules:
  0.0 308.9 jit_solution(166592716257265066)
XLA Ops:
  0.0 1.8 copy.97
  1.9 10.7 %collective-permute-start = (f32[64,1,512]{2,0,1:T(8,128)S(1)}, f32[64,1,512]{2,0,1:T(8,128)S(1)}, u32[]{:S(2)}, u32[]{:S(2)}) collective-permute-start(f32[64,1,512]{2,0,1:T(8,128)S(1)} %get-tuple-element.17), channel_id=1, source_target_pairs={{1,0},{2,1},{3,2},{4,3},{5,4},{6,5},{7,6},{8,7},{9,8},{10,9},{11,1... | collective-permute-start | bytes 393224 | tf_op jit(solution)/shard_map/ppermute | solution.py:23
  12.6 1.9 collective-permute-start.1
  15.1 16.3 %collective-permute-done.1 = f32[64,1,512]{2,0,1:T(8,128)S(1)} collective-permute-done((f32[64,1,512]{2,0,1:T(8,128)S(1)}, f32[64,1,512]{2,0,1:T(8,128)S(1)}, u32[]{:S(2)}, u32[]{:S(2)}) %collective-permute-start.1) | collective-permute-done | bytes 131104 | tf_op jit(solution)/shard_map/ppermute | solution.py:20
  31.4 0.7 multiply_add_fusion.1
  32.4 1.9 collective-permute-start.2
  34.4 3.4 %collective-permute-start.3 = (f32[64,1,512]{2,0,1:T(8,128)S(1)}, f32[64,1,512]{2,0,1:T(8,128)S(1)}, u32[]{:S(2)}, u32[]{:S(2)}) collective-permute-start(f32[64,1,512]{2,0,1:T(8,128)S(1)} %get-tuple-element.10), channel_id=1, source_target_pairs={{0,1},{1,2},{2,3},{3,4},{4,5},{5,6},{6,7},{7,8},{8,9},{9,10},{10,1... | collective-permute-start | bytes 393224 | tf_op jit(solution)/shard_map/ppermute | solution.py:20
  38.2 15.0 %collective-permute-done.3 = f32[64,1,512]{2,0,1:T(8,128)S(1)} collective-permute-done((f32[64,1,512]{2,0,1:T(8,128)S(1)}, f32[64,1,512]{2,0,1:T(8,128)S(1)}, u32[]{:S(2)}, u32[]{:S(2)}) %collective-permute-start.3) | collective-permute-done | bytes 131104 | tf_op jit(solution)/shard_map/ppermute | solution.py:20
  53.2 0.7 multiply_add_fusion
  53.9 0.6 copy.103
  54.7 1.6 copy.104
  56.3 18.3 %all-to-all-start = ((f32[64,16,256]{2,0,1:T(8,128)}), f32[64,16,256]{2,0,1:T(8,128)S(1)}, u32[]{:S(2)}, u32[]{:S(2)}) async-start(f32[64,16,256]{2,0,1:T(8,128)} %copy.104), calls=%async_computation | async-start | bytes 2097152 | tf_op jit(solution)/shard_map/all_to_all | solution.py:95
  74.8 1.3 slice.96
  76.1 1.0 reshape.83
  77.1 1.4 pad_maximum_fusion.8
  78.5 1.6 copy.109
  80.1 1.3 reshape.85
  81.4 0.6 copy.110
  82.1 0.6 copy-done.1
  82.7 0.6 copy.107
  83.3 2.0 gather_fusion.1
  85.3 2.0 gather_fusion
  87.3 3.9 %select_bitcast_fusion = (f32[64,64,128]{2,0,1:T(8,128)}, f32[64,64,128]{2,0,1:T(8,128)S(1)}) fusion(f32[64,64,128]{2,1,0:T(8,128)} %gather_fusion.1, pred[64]{0:T(512)(128)(4,1)S(1)} %compare_and_fusion, f32[64,64,128]{2,1,0:T(8,128)} %gather_fusion), kind=kLoop, calls=%fused_computation.10 | loop fusion | flops 1048576 | bytes 8388672 | tf_op jit(solution)/shard_map/jit(_take)/select_n | solution.py:91
  91.2 2.6 copy.108
  93.7 1.7 reshape.84
  95.5 4.1 %copy.111 = f32[64,64,128]{2,1,0:T(8,128)} copy(f32[64,64,128]{2,0,1:T(8,128)} %get-tuple-element.20) | data formatting | bytes 4194304 | tf_op jit(solution)/shard_map/jit(_take)/select_n | solution.py:91
  99.6 2.7 reshape.86
  102.4 2.1 multiply_select_fusion
  104.5 2.6 copy.112
  107.0 12.8 %all-to-all-done = f32[64,16,256]{2,0,1:T(8,128)S(1)} async-done(((f32[64,16,256]{2,0,1:T(8,128)}), f32[64,16,256]{2,0,1:T(8,128)S(1)}, u32[]{:S(2)}, u32[]{:S(2)}) %all-to-all-start) | async-done | bytes 1048608 | tf_op jit(solution)/shard_map/all_to_all | solution.py:95
  119.8 10.3 %all-to-all-start.1 = ((f32[64,16,512]{2,0,1:T(8,128)}), f32[64,16,512]{2,0,1:T(8,128)S(1)}, u32[]{:S(2)}, u32[]{:S(2)}) async-start(f32[64,16,512]{2,0,1:T(8,128)} %copy.112), calls=%async_computation.1 | async-start | bytes 4194304 | tf_op jit(solution)/shard_map/all_to_all | solution.py:96
  130.3 88.3 %all-to-all-done.1 = f32[64,16,512]{2,0,1:T(8,128)S(1)} async-done(((f32[64,16,512]{2,0,1:T(8,128)}), f32[64,16,512]{2,0,1:T(8,128)S(1)}, u32[]{:S(2)}, u32[]{:S(2)}) %all-to-all-start.1) | async-done | bytes 2097184 | tf_op jit(solution)/shard_map/all_to_all | solution.py:96
  218.8 3.6 %abs_reduce_fusion = (f32[512]{0:T(512)S(1)}, f32[512,512]{0,1:T(8,128)S(1)}) fusion(f32[512]{0:T(512)S(1)} %bitcast.106, f32[64,16,512]{2,0,1:T(8,128)S(1)} %all-to-all-done.1, f32[512]{0:T(512)S(1)} %get-tuple-element.19), kind=kOutput, calls=%fused_computation.40 | convolution fusion | flops 3223322112 | bytes 3151872 | tf_op jit(solution)/shard_map/dot_general | solution.py:43
  222.4 3.5 %fusion.8 = f32[512,512]{1,0:T(8,128)S(1)} fusion(f32[512,512]{0,1:T(8,128)S(1)} %get-tuple-element.23, f32[512]{0:T(512)S(1)} %broadcast_divide_fusion), kind=kOutput, calls=%fused_computation.15 | convolution fusion | flops 1611137024 | bytes 2099200 | tf_op jit(solution)/shard_map/dot_general | solution.py:57
  226.0 1.9 fusion.10
  227.9 3.7 %fusion.46 = f32[512,512]{1,0:T(8,128)S(1)} fusion(f32[512,512]{0,1:T(8,128)S(1)} %get-tuple-element.23, f32[512,512]{0,1:T(8,128)S(1)} %fusion.10), kind=kOutput, calls=%fused_computation.67 | convolution fusion | flops 1610612736 | bytes 3145728 | tf_op jit(solution)/shard_map/dot_general | solution.py:57
  231.6 1.9 convolution_subtract_fusion.2
  233.5 3.6 %fusion.47 = f32[512,512]{1,0:T(8,128)S(1)} fusion(f32[512,512]{0,1:T(8,128)S(1)} %get-tuple-element.23, f32[512,512]{0,1:T(8,128)S(1)} %convolution_subtract_fusion.2), kind=kOutput, calls=%fused_computation.68 | convolution fusion | flops 1610612736 | bytes 3145728 | tf_op jit(solution)/shard_map/dot_general | solution.py:57
  237.1 1.9 convolution_subtract_fusion.1
  239.0 3.6 %fusion.48 = f32[512,512]{1,0:T(8,128)S(1)} fusion(f32[512,512]{0,1:T(8,128)S(1)} %get-tuple-element.23, f32[512,512]{0,1:T(8,128)S(1)} %convolution_subtract_fusion.1), kind=kOutput, calls=%fused_computation.69 | convolution fusion | flops 1610612736 | bytes 3145728 | tf_op jit(solution)/shard_map/dot_general | solution.py:57
  242.5 2.1 convolution_subtract_fusion
  244.7 2.0 fusion.26
  246.7 1.1 fusion.49
  248.1 1.9 fusion.22
  249.9 1.1 copy.119
  251.0 55.8 %all_to_all.45 = f32[1024,1,256]{2,1,0:T(1,128)S(1)} all-to-all(f32[1024,1,256]{2,1,0:T(1,128)S(1)} %copy.119), channel_id=1, replica_groups=mesh['mem'=16,'lat'=32] {'mem'}, dimensions={0} | all-to-all | bytes 2097152 | tf_op jit(solution)/shard_map/all_to_all | solution.py:112
  306.8 0.6 copy.120
  307.4 1.3 reshape.89
  (38 shorter events, 2.4 us)
Async XLA Ops:
  1.9 13.2 %collective-permute-start = (f32[64,1,512]{2,0,1:T(8,128)S(1)}, f32[64,1,512]{2,0,1:T(8,128)S(1)}, u32[]{:S(2)}, u32[]{:S(2)}) collective-permute-start(f32[64,1,512]{2,0,1:T(8,128)S(1)} %get-tuple-element.17), channel_id=1, source_target_pairs={{1,0},{2,1},{3,2},{4,3},{5,4},{6,5},{7,6},{8,7},{9,8},{10,9},{11,1... | collective-permute-start | bytes 393224 | tf_op jit(solution)/shard_map/ppermute | solution.py:23
  12.6 18.8 %copy-start.2 = (f32[8,512]{1,0:T(8,128)S(1)}, f32[8,512]{1,0:T(8,128)}, u32[]{:S(2)}) copy-start(f32[8,512]{1,0:T(8,128)} %param.10) | copy-start | bytes 49156
  12.6 18.8 %copy-start.3 = (f32[8,512]{1,0:T(8,128)S(1)}, f32[8,512]{1,0:T(8,128)}, u32[]{:S(2)}) copy-start(f32[8,512]{1,0:T(8,128)} %param.11) | copy-start | bytes 49156
  12.6 18.7 %collective-permute-start.1 = (f32[64,1,512]{2,0,1:T(8,128)S(1)}, f32[64,1,512]{2,0,1:T(8,128)S(1)}, u32[]{:S(2)}, u32[]{:S(2)}) collective-permute-start(f32[64,1,512]{2,0,1:T(8,128)S(1)} %get-tuple-element.16), channel_id=1, source_target_pairs={{0,1},{1,2},{2,3},{3,4},{4,5},{5,6},{6,7},{7,8},{8,9},{9,10},{10,1... | collective-permute-start | bytes 393224 | tf_op jit(solution)/shard_map/ppermute | solution.py:20
  32.4 5.7 %collective-permute-start.2 = (f32[64,1,512]{2,0,1:T(8,128)S(1)}, f32[64,1,512]{2,0,1:T(8,128)S(1)}, u32[]{:S(2)}, u32[]{:S(2)}) collective-permute-start(f32[64,1,512]{2,0,1:T(8,128)S(1)} %get-tuple-element.11), channel_id=1, source_target_pairs={{1,0},{2,1},{3,2},{4,3},{5,4},{6,5},{7,6},{8,7},{9,8},{10,9},{11,1... | collective-permute-start | bytes 393224 | tf_op jit(solution)/shard_map/ppermute | solution.py:23
  34.4 18.8 %collective-permute-start.3 = (f32[64,1,512]{2,0,1:T(8,128)S(1)}, f32[64,1,512]{2,0,1:T(8,128)S(1)}, u32[]{:S(2)}, u32[]{:S(2)}) collective-permute-start(f32[64,1,512]{2,0,1:T(8,128)S(1)} %get-tuple-element.10), channel_id=1, source_target_pairs={{0,1},{1,2},{2,3},{3,4},{4,5},{5,6},{6,7},{7,8},{8,9},{9,10},{10,1... | collective-permute-start | bytes 393224 | tf_op jit(solution)/shard_map/ppermute | solution.py:20
  53.9 22.2 %copy-start = (f32[64,8,512]{2,0,1:T(8,128)}, f32[64,8,512]{2,0,1:T(8,128)S(1)}, u32[]{:S(2)}) copy-start(f32[64,8,512]{2,0,1:T(8,128)S(1)} %multiply_add_fusion) | copy-start | bytes 3145732
  54.6 19.9 %copy-start.5 = (s32[1,16,4]{1,2,0:T(4,128)S(1)}, s32[1,16,4]{1,2,0:T(4,128)}, u32[]{:S(2)}) copy-start(s32[1,16,4]{1,2,0:T(4,128)} %param.12) | copy-start | bytes 772
  54.7 20.1 %copy-start.4 = (s32[1,16,512]{2,1,0:T(8,128)S(1)}, s32[1,16,512]{2,1,0:T(8,128)}, u32[]{:S(2)}) copy-start(s32[1,16,512]{2,1,0:T(8,128)} %param.13) | copy-start | bytes 98308
  56.3 63.5 %all-to-all-start = ((f32[64,16,256]{2,0,1:T(8,128)}), f32[64,16,256]{2,0,1:T(8,128)S(1)}, u32[]{:S(2)}, u32[]{:S(2)}) async-start(f32[64,16,256]{2,0,1:T(8,128)} %copy.104), calls=%async_computation | async-start | bytes 2097152 | tf_op jit(solution)/shard_map/all_to_all | solution.py:95
  76.1 1.1 slice-start
  81.4 1.2 copy-start.1
  119.8 98.8 %all-to-all-start.1 = ((f32[64,16,512]{2,0,1:T(8,128)}), f32[64,16,512]{2,0,1:T(8,128)S(1)}, u32[]{:S(2)}, u32[]{:S(2)}) async-start(f32[64,16,512]{2,0,1:T(8,128)} %copy.112), calls=%async_computation.1 | async-start | bytes 4194304 | tf_op jit(solution)/shard_map/all_to_all | solution.py:96
  130.1 88.6 %copy-start.6 = (f32[1,1,512]{2,1,0:T(1,128)S(1)}, f32[1,1,512]{2,1,0:T(1,128)}, u32[]{:S(2)}) copy-start(f32[1,1,512]{2,1,0:T(1,128)} %param.14) | copy-start | bytes 6148
  130.2 88.6 %copy-start.7 = (f32[1,1,512]{2,1,0:T(1,128)S(1)}, f32[1,1,512]{2,1,0:T(1,128)}, u32[]{:S(2)}) copy-start(f32[1,1,512]{2,1,0:T(1,128)} %param.15) | copy-start | bytes 6148
where the time goes:
time: 314 us; the launch traced here: 309 us
  waiting for transfers between devices  133 us (42%)
  blocking collectives  55.8 us (18%)
  starting transfers between devices  46.5 us (15%)
  local copies, waits for them, and re-layouts  33.3 us (11%)
  matrix products  30.7 us (10%)
  other arithmetic  9.4 us (3%)
    all_to_all x1, waiting for transfers between devices, body(): lax.all_to_all(observed, 'mem', split_axis=1, concat_axis=0, tiled=True)  88.3 us
    all_to_all x1, blocking collectives, body(): lax.all_to_all(analysed, 'mem', split_axis=0, concat_axis=1, tiled=True)  55.8 us
    ppermute x2, waiting for transfers between devices, with_halo(): lax.ppermute(lax.slice_in_dim(block, block.shape[dim] - width, None, axis...  31.3 us
    all_to_all x1, starting transfers between devices, body(): lax.all_to_all(owned, 'mem', split_axis=1, concat_axis=0, tiled=True)  18.3 us
    dot_general x4, matrix products, patch_gain(): jnp.dot(covariance, inverse, precision=HIGHEST, preferred_element_type=jn...  14.4 us
    all_to_all x1, waiting for transfers between devices, body(): lax.all_to_all(owned, 'mem', split_axis=1, concat_axis=0, tiled=True)  12.8 us
    ppermute x2, starting transfers between devices, with_halo(): lax.ppermute(lax.slice_in_dim(block, 0, width, axis=dim), axis, backward)  12.6 us
    all_to_all x1, starting transfers between devices, body(): lax.all_to_all(observed, 'mem', split_axis=1, concat_axis=0, tiled=True)  10.3 us
  transfers between devices with their start and end apart: 6, of which 5 were waited for; matrix products, arithmetic and copies ran while one was open for 11% of the time, Pallas kernels for 0%

commit v1 on v0

v1 whole, which is shorter than its diff:
```python
import jax
import jax.numpy as jnp
from jax import lax
from jax.experimental import pallas as pl
from jax.experimental.pallas import tpu as pltpu
from jax.sharding import PartitionSpec as P

MESH = pl.DeviceIdType.MESH
BOTH = ("mem", "lat")
ADVECTION = 0.1
CHUNKS = 4
MEMBERS = 64
ROWS = MEMBERS // CHUNKS
PREC = lax.Precision.HIGH


def m8(v):
    return (v + 16) % 8


def device(z, c, h, s, w):
    return (z * 2 + c, h * 16 + (w // 2) * 4 + s * 2 + w % 2)


def place():
    m, l = lax.axis_index("mem"), lax.axis_index("lat")
    return m // 2, m % 2, l // 16, (l % 4) // 2, ((l // 4) % 4) * 2 + l % 2


def to_plane():
    pairs = []
    for m in range(16):
        for l in range(32):
            z, c, h, s, w = m // 2, m % 2, l // 16, (l % 4) // 2, ((l // 4) % 4) * 2 + l % 2
            a, b = device(w, c, h, s, m8(w - z + 4 * c))
            pairs.append((m * 32 + l, a * 32 + b))
    return pairs


def enter(peers, others):
    barrier = pltpu.get_barrier_semaphore()

    @pl.loop(1, 16)
    def _(i):
        pl.semaphore_signal(barrier, inc=1, device_id=peers(i), device_id_type=MESH)

    (first, second), there = others

    @pl.when(there)
    def _():
        pl.semaphore_signal(barrier, inc=1, device_id=first, device_id_type=MESH)
        pl.semaphore_signal(barrier, inc=1, device_id=second, device_id_type=MESH)
        pl.semaphore_wait(barrier, 17)

    @pl.when(jnp.logical_not(there))
    def _():
        pl.semaphore_wait(barrier, 15)


class Move:
    def __init__(self, source, target, send, recv, where, away):
        self.away, self.home = away, jnp.logical_not(away)
        self.remote = pltpu.make_async_remote_copy(
            source, target, send, recv, device_id=where, device_id_type=MESH
        )
        self.local = pltpu.make_async_copy(source, target, recv)

    def start(self):
        pl.when(self.away)(self.remote.start)
        pl.when(self.home)(self.local.start)

    def wait_recv(self):
        pl.when(self.away)(self.remote.wait_recv)
        pl.when(self.home)(self.local.wait)

    def wait_send(self):
        pl.when(self.away)(self.remote.wait_send)


def gather_kernel(blocks, nexts, flags, field, out, *scratch):
    near, far, stage = scratch[:CHUNKS], scratch[CHUNKS : 2 * CHUNKS], scratch[2 * CHUNKS : 3 * CHUNKS]
    spread_send, spread_recv, hop_send, hop_recv, send, recv = scratch[3 * CHUNKS :]
    z, c, h, s, w = place()
    mine = w * 2 + c
    patch = m8(z - w + 4 * c) * 2 + c

    def peer(i):
        k = (mine + i) % 16
        return k, device(z, k % 2, h, s, k // 2)

    hop_to, hop_from = device(m8(w + z - 4 * c), c, h, s, w), device(m8(z - w + 4 * c), c, h, s, w)
    hops = m8(w - 4 * c) != 0
    enter(lambda i: peer(i)[1], ((hop_to, hop_from), hops))

    spread_to = device(z, c, h, s, m8(w - z + 4 * c))
    spreads = m8(4 * c - z) != 0
    spread = [
        Move(field.at[:, pl.ds(i * ROWS, ROWS)], near[i], spread_send.at[i], spread_recv.at[i], spread_to, spreads)
        for i in range(CHUNKS)
    ]
    hop = [Move(near[i], far[i], hop_send.at[i], hop_recv.at[i], hop_to, hops) for i in range(CHUNKS)]

    def piece(i, off):
        k, where = peer(off)
        wanted = m8(z - k // 2 + 4 * (k % 2)) * 2 + k % 2
        return pltpu.make_async_remote_copy(
            stage[i].at[wanted],
            out.at[mine, pl.ds(i * ROWS, ROWS)],
            send.at[i, off],
            recv.at[i, off],
            device_id=where,
            device_id_type=MESH,
        )

    def own(i):
        return pltpu.make_async_copy(stage[i].at[patch], out.at[mine, pl.ds(i * ROWS, ROWS)], recv.at[i, 0])

    first_lane = lax.broadcasted_iota(jnp.int32, (ROWS, 128), 1) == 0

    def observe(i):
        hop[i].wait_recv()
        tiles, put = far[i], stage[i]

        @pl.loop(0, 16)
        def _(p):
            for t in range(2):
                put[p, :, t * 128 : (t + 1) * 128] = tiles[2 * p + t]
            for j in range(4):
                direct = tiles[blocks[p * 4 + j]]
                beside = jnp.where(first_lane, tiles[nexts[p * 4 + j]], direct)
                east = pltpu.roll(beside, 127, 1)
                seen = jnp.where(flags[p * 4 + j] == 1, 0.5 * (direct + east), direct)
                put[p, :, 256 + j * 128 : 384 + j * 128] = seen

        @pl.loop(1, 16)
        def _(off):
            piece(i, off).start()

        own(i).start()

    for i in range(CHUNKS):
        spread[i].start()
    for i in range(CHUNKS):
        spread[i].wait_recv()
        hop[i].start()
        if i > 0:
            observe(i - 1)
    observe(CHUNKS - 1)
    for i in range(CHUNKS):

        @pl.loop(1, 16)
        def _(off):
            piece(i, off).wait()

        own(i).wait()
        spread[i].wait_send()
        hop[i].wait_send()


def gather(field, blocks, nexts, flags):
    chunk = pltpu.VMEM((32, ROWS, 128), jnp.float32)
    dma = pltpu.SemaphoreType.DMA
    vmem, smem = pl.BlockSpec(memory_space=pltpu.VMEM), pl.BlockSpec(memory_space=pltpu.SMEM)
    return pl.pallas_call(
        gather_kernel,
        out_shape=jax.ShapeDtypeStruct((16, MEMBERS, 768), jnp.float32),
        in_specs=[smem, smem, vmem, vmem],
        out_specs=vmem,
        scratch_shapes=[chunk] * (2 * CHUNKS)
        + [pltpu.VMEM((16, ROWS, 768), jnp.float32)] * CHUNKS
        + [dma((CHUNKS,))] * 4
        + [dma((CHUNKS, 16))] * 2,
        compiler_params=pltpu.CompilerParams(
            collective_id=0, has_side_effects=True, vmem_limit_bytes=40 * 2**20
        ),
        name="gather",
    )(blocks, nexts, flags, field)


def scatter_kernel(cells, out, *scratch):
    held = scratch[:CHUNKS]
    home_send, home_recv, send, recv = scratch[CHUNKS:]
    z, c, h, s, w = place()
    mine = w * 2 + c
    patch = m8(z - w + 4 * c) * 2 + c

    def peer(i):
        k = (mine + i) % 16
        return k, device(z, k % 2, h, s, k // 2)

    home, guest = device(m8(z - w + 4 * c), c, h, s, z), device(w, c, h, s, m8(w - z + 4 * c))
    away = jnp.logical_or(w != z, m8(z - w + 4 * c) != z)
    enter(lambda i: peer(i)[1], ((home, guest), away))

    def piece(i, off):
        k, where = peer(off)
        return pltpu.make_async_remote_copy(
            cells.at[k, pl.ds(i * ROWS, ROWS)],
            held[i].at[patch],
            send.at[i, off],
            recv.at[i, off],
            device_id=where,
            device_id_type=MESH,
        )

    def own(i):
        return pltpu.make_async_copy(cells.at[mine, pl.ds(i * ROWS, ROWS)], held[i].at[patch], recv.at[i, 0])

    back = [
        Move(held[i], out.at[:, pl.ds(i * ROWS, ROWS)], home_send.at[i], home_recv.at[i], home, away)
        for i in range(CHUNKS)
    ]
    for i in range(CHUNKS):

        @pl.loop(1, 16)
        def _(off):
            piece(i, off).start()

        own(i).start()
    for i in range(CHUNKS):

        @pl.loop(1, 16)
        def _(off):
            piece(i, off).wait()

        own(i).wait()
        back[i].start()
    for i in range(CHUNKS):
        back[i].wait_recv()
        back[i].wait_send()


def scatter(cells):
    dma = pltpu.SemaphoreType.DMA
    vmem = pl.BlockSpec(memory_space=pltpu.VMEM)
    return pl.pallas_call(
        scatter_kernel,
        out_shape=jax.ShapeDtypeStruct((16, MEMBERS, 256), jnp.float32),
        in_specs=[vmem],
        out_specs=vmem,
        scratch_shapes=[pltpu.VMEM((16, ROWS, 256), jnp.float32)] * CHUNKS
        + [dma((CHUNKS,))] * 2
        + [dma((CHUNKS, 16))] * 2,
        compiler_params=pltpu.CompilerParams(
            collective_id=1, has_side_effects=True, vmem_limit_bytes=40 * 2**20
        ),
        name="scatter",
    )(cells)


def advance(padded, diffusivity, north_wind):
    centre, northern, southern = padded[1:-1], padded[:-2], padded[2:]
    eastern = jnp.roll(centre, -1, axis=2)
    western = jnp.roll(centre, 1, axis=2)
    return (
        centre
        - ADVECTION * centre * (eastern - western)
        - north_wind * (southern - northern)
        + diffusivity * (eastern + western + northern + southern - 4.0 * centre)
    )


def forecast(ensemble, diffusivity, north_wind):
    bands = lax.axis_size("lat")
    ahead = [(i, i + 1) for i in range(bands - 1)]
    behind = [(i + 1, i) for i in range(bands - 1)]
    field = ensemble.transpose(1, 0, 2)
    terms = jnp.stack([diffusivity, north_wind], axis=1)

    def edge(first, last, field_rows, term_rows):
        del first, last
        return jnp.concatenate([field_rows.reshape(-1, 512), term_rows.reshape(-1, 512)])

    count = 2 * field.shape[1]
    low = lax.ppermute(edge(0, 0, field[-2:], terms[-1:]), "lat", ahead)
    high = lax.ppermute(edge(0, 0, field[:2], terms[:1]), "lat", behind)
    padded = jnp.concatenate(
        [low[:count].reshape(2, -1, 512), field, high[:count].reshape(2, -1, 512)]
    )
    terms = jnp.concatenate([low[count:][None], terms, high[count:][None]])
    band = lax.axis_index("lat")
    row = lax.broadcasted_iota(jnp.int32, (10, 1, 1), 0)
    inside = jnp.logical_and(
        jnp.logical_or(row > 0, band > 0), jnp.logical_or(row < 9, band < bands - 1)
    )
    once = advance(padded, terms[:, 0:1], terms[:, 1:2])
    once = jnp.where(inside, once, 0.0)
    return advance(once, terms[1:-1, 0:1], terms[1:-1, 1:2])


def dot(left, right):
    return jnp.dot(left, right, precision=PREC, preferred_element_type=jnp.float32)


def analyse(states, values, errors):
    count = states.shape[0]
    mean = jnp.mean(states, axis=0)
    offset = states - mean
    seen_offset = offset[:, 256:]
    products = lax.dot_general(
        offset, seen_offset, (((0,), (0,)), ((), ())), precision=PREC, preferred_element_type=jnp.float32
    ) / (count - 1.0)
    covariance = products[256:] + jnp.diag(errors)
    scale = lax.rsqrt(jnp.sum(jnp.abs(covariance), axis=1))
    power = jnp.eye(512, dtype=jnp.float32) - covariance * scale[:, None] * scale[None, :]
    gain = products[:256] * scale[None, :]
    for step in range(4):
        gain = gain + dot(gain, power)
        if step < 3:
            power = dot(power, power)
    gain = gain * scale[None, :]
    weights = (values - mean[256:])[None, :] - 0.5 * seen_offset
    update = lax.dot_general(
        weights, gain, (((1,), (1,)), ((), ())), precision=PREC, preferred_element_type=jnp.float32
    )
    return states[:, :256] + update


def body(ensemble, diffusivity, north_wind, observed_blocks, eastern_average_flags, observed_values, observed_error):
    small = jnp.concatenate(
        [
            eastern_average_flags[0].astype(jnp.float32),
            observed_values[0],
            observed_error[0],
            jnp.pad(observed_blocks[0].reshape(1, 64).astype(jnp.float32), ((0, 0), (0, 448))),
        ]
    )
    small = lax.ppermute(small, BOTH, to_plane())
    flags = small[:16].astype(jnp.int32).reshape(64, 1, 128)
    values, errors = small[16], small[17]
    blocks = small[18, :64].astype(jnp.int32)
    nexts = blocks - blocks % 4 + (blocks + 1) % 4
    field = forecast(ensemble, diffusivity, north_wind)
    field = field.reshape(8, MEMBERS, 4, 128).transpose(0, 2, 1, 3).reshape(32, MEMBERS, 128)
    states = gather(field, blocks, nexts, flags).reshape(16 * MEMBERS, 768)
    cells = analyse(states, values, errors).reshape(16, MEMBERS, 256)
    out = scatter(cells)
    return out.reshape(8, 2, MEMBERS, 256).transpose(2, 0, 1, 3).reshape(MEMBERS, 8, 512)


def solution(mesh):
    return jax.shard_map(
        body,
        mesh=mesh,
        in_specs=(
            P("mem", "lat", None),
            P("lat", None),
            P("lat", None),
            P("lat", None, None),
            P("lat", None, None),
            P("lat", "mem", None),
            P("lat", "mem", None),
        ),
        out_specs=P("mem", "lat", None),
        check_vma=False,
    )
```

time: 314 us -> 239 us (0.76)
  the two profiles are of different devices: /device:TPU:481 before, /device:TPU:419 now
where the time goes in v1:
time: 239 us; the launch traced here: 238 us
  Pallas kernels  193 us (81%)
  starting transfers between devices  12 us (5%)
  matrix products  12 us (5%)
  waiting for transfers between devices  7.18 us (3%)
  other arithmetic  7.01 us (3%)
  local copies, waits for them, and re-layouts  6.52 us (3%)
    pallas_call x1, Pallas kernels, gather(): pl.pallas_call(gather_kernel, out_shape=jax.ShapeDtypeStruct((16, MEMBERS...  116 us
    pallas_call x1, Pallas kernels, scatter(): pl.pallas_call(scatter_kernel, out_shape=jax.ShapeDtypeStruct((16, MEMBER...  77.2 us
    dot_general x7, matrix products, dot(): jnp.dot(left, right, precision=PREC, preferred_element_type=jnp.float32)  7.85 us
    ppermute x1, starting transfers between devices, body(): small = lax.ppermute(small, BOTH, to_plane())  5.72 us
    ppermute x1, waiting for transfers between devices, forecast(): low = lax.ppermute(edge(0, 0, field[-2:], terms[-1:]), 'lat', ahead)  5.48 us
  transfers between devices with their start and end apart: 3, of which 2 were waited for; matrix products, arithmetic and copies ran while one was open for 1% of the time, Pallas kernels for 0%

profile of v1, /device:TPU:419, one launch (start us, length us, event | category | flops | bytes accessed | tf_op | source)
XLA Modules:
  0.0 238.3 jit_solution(15027476848325173364)
XLA Ops:
  0.0 0.7 convert_element_type.35
  0.7 0.1 copy.22
  0.8 0.1 convert_element_type.36
  0.9 0.8 convert_bitcast_fusion
  1.6 0.7 select_maximum_fusion
  2.3 5.7 %collective-permute-start = (f32[19,512]{1,0:T(8,128)S(1)}, f32[19,512]{1,0:T(8,128)S(1)}, u32[]{:S(2)}, u32[]{:S(2)}) collective-permute-start(f32[19,512]{1,0:T(8,128)S(1)} %select_maximum_fusion), channel_id=1, source_target_pairs={{0,0},{1,65},{2,2},{3,67},{4,132},{5,197},{6,134},{7,199},{8,264},... | collective-permute-start | bytes 116744 | tf_op jit(solution)/shard_map/ppermute | solution.py:328
  8.1 0.8 pad_maximum_fusion.12
  8.9 1.9 fusion.47
  10.8 0.0 copy-start
  10.8 0.1 copy.25
  10.9 4.4 %collective-permute-start.2 = (f32[130,512]{1,0:T(8,128)S(1)}, f32[130,512]{1,0:T(8,128)S(1)}, u32[]{:S(2)}, u32[]{:S(2)}) collective-permute-start(f32[130,512]{1,0:T(8,128)S(1)} %pad_maximum_fusion.9), channel_id=1, source_target_pairs={{1,0},{2,1},{3,2},{4,3},{5,4},{6,5},{7,6},{8,7},{9,8},{10,9},{11,1... | collective-permute-start | bytes 798728 | tf_op jit(solution)/shard_map/ppermute | solution.py:276
  15.3 0.1 copy.23
  15.4 1.9 collective-permute-start.1
  17.3 0.0 collective-permute-done
  17.4 1.7 collective-permute-done.2
  19.2 0.2 copy.28
  19.4 5.5 %collective-permute-done.1 = f32[130,512]{1,0:T(8,128)S(1)} collective-permute-done((f32[130,512]{1,0:T(8,128)S(1)}, f32[130,512]{1,0:T(8,128)S(1)}, u32[]{:S(2)}, u32[]{:S(2)}) %collective-permute-start.1) | collective-permute-done | bytes 266272 | tf_op jit(solution)/shard_map/ppermute | solution.py:275
  24.9 0.2 copy.27
  25.1 0.0 copy-done
  25.1 0.4 pad_maximum_fusion
  25.5 0.2 fusion.45
  25.7 0.0 copy-start.1
  25.7 0.0 copy-start.2
  25.8 1.0 fusion.44
  26.9 0.0 copy-done.1
  26.9 0.0 copy-done.2
  26.9 2.1 fusion.5
  29.0 0.2 fusion.43
  29.2 0.5 fusion.42
  29.7 0.8 multiply_add_fusion
  30.5 0.1 fusion.46
  30.6 0.1 pad_maximum_fusion.7
  30.6 0.2 copy.31
  30.9 115.8 %gather.1 = f32[16,64,768]{2,1,0:T(8,128)S(1)} custom-call(s32[64]{0:T(128)S(1)} %fusion.38.blocks, s32[64]{0:T(128)S(1)} %fusion.35.nexts, s32[64,1,128]{2,1,0:T(1,128)S(1)} %reshape.81.flags, f32[32,64,128]{2,1,0:T(8,128)S(1)} %bitcast.48), custom_call_target="tpu_custom_call" | custom-call | tf_op jit(solution)/shard_map/gather/pallas_call | solution.py:164
  146.7 0.2 reduce_sum.18
  147.0 0.2 broadcast_subtract_fusion
  147.2 3.2 %fusion.15 = f32[768,512]{0,1:T(8,128)S(1)} fusion(f32[1024,768]{1,0:T(8,128)S(1)} %broadcast_subtract_fusion), kind=kOutput, calls=%fused_computation.21 | convolution fusion | flops 2416312320 | bytes 6815744 | tf_op jit(solution)/shard_map/dot_general | solution.py:300
  150.3 0.2 abs_reduce_fusion
  150.5 0.7 convolution_add_fusion.3
  151.2 2.1 fusion.24
  153.4 1.0 fusion.49
  154.4 1.0 convolution_add_fusion.2
  155.4 1.0 fusion.50
  156.4 1.0 convolution_add_fusion.1
  157.4 1.0 fusion.21
  158.4 1.0 fusion.18
  159.5 77.2 %scatter.1 = f32[16,64,256]{2,1,0:T(8,128)S(1)} custom-call(f32[16,64,256]{2,1,0:T(8,128)S(1)} %bitcast.50), custom_call_target="tpu_custom_call" | custom-call | tf_op jit(solution)/shard_map/scatter/pallas_call | solution.py:236
  236.7 1.6 copy.35
  (21 shorter events, 0.2 us)
Async XLA Ops:
  2.3 15.0 %collective-permute-start = (f32[19,512]{1,0:T(8,128)S(1)}, f32[19,512]{1,0:T(8,128)S(1)}, u32[]{:S(2)}, u32[]{:S(2)}) collective-permute-start(f32[19,512]{1,0:T(8,128)S(1)} %select_maximum_fusion), channel_id=1, source_target_pairs={{0,0},{1,65},{2,2},{3,67},{4,132},{5,197},{6,134},{7,199},{8,264},... | collective-permute-start | bytes 116744 | tf_op jit(solution)/shard_map/ppermute | solution.py:328
  10.8 14.3 %copy-start = (f32[64,8,512]{2,1,0:T(8,128)S(1)}, f32[64,8,512]{2,1,0:T(8,128)}, u32[]{:S(2)}) copy-start(f32[64,8,512]{2,1,0:T(8,128)} %param.7) | copy-start | bytes 3145732
  10.9 8.3 %collective-permute-start.2 = (f32[130,512]{1,0:T(8,128)S(1)}, f32[130,512]{1,0:T(8,128)S(1)}, u32[]{:S(2)}, u32[]{:S(2)}) collective-permute-start(f32[130,512]{1,0:T(8,128)S(1)} %pad_maximum_fusion.9), channel_id=1, source_target_pairs={{1,0},{2,1},{3,2},{4,3},{5,4},{6,5},{7,6},{8,7},{9,8},{10,9},{11,1... | collective-permute-start | bytes 798728 | tf_op jit(solution)/shard_map/ppermute | solution.py:276
  15.4 9.5 %collective-permute-start.1 = (f32[130,512]{1,0:T(8,128)S(1)}, f32[130,512]{1,0:T(8,128)S(1)}, u32[]{:S(2)}, u32[]{:S(2)}) collective-permute-start(f32[130,512]{1,0:T(8,128)S(1)} %pad_maximum_fusion.8), channel_id=1, source_target_pairs={{0,1},{1,2},{2,3},{3,4},{4,5},{5,6},{6,7},{7,8},{8,9},{9,10},{10,1... | collective-permute-start | bytes 798728 | tf_op jit(solution)/shard_map/ppermute | solution.py:275
  25.7 1.1 copy-start.1
  25.7 1.1 copy-start.2

commit v2 on v1

v2 whole, which is shorter than its diff:
```python
import jax
import jax.numpy as jnp
from jax import lax
from jax.experimental import pallas as pl
from jax.experimental.pallas import tpu as pltpu
from jax.sharding import PartitionSpec as P

MESH = pl.DeviceIdType.MESH
ADVECTION = 0.1
CHUNKS = 4
MEMBERS = 64
ROWS = MEMBERS // CHUNKS
PREC = lax.Precision.HIGH


def m8(v):
    return (v + 16) % 8


def device(z, c, h, s, w):
    return (z * 2 + c, h * 16 + (w // 2) * 4 + s * 2 + w % 2)


def place():
    m, l = lax.axis_index("mem"), lax.axis_index("lat")
    return m // 2, m % 2, l // 16, (l % 4) // 2, ((l // 4) % 4) * 2 + l % 2


def enter(peers, sources, targets):
    barrier = pltpu.get_barrier_semaphore()

    @pl.loop(1, 16)
    def _(i):
        pl.semaphore_signal(barrier, inc=1, device_id=peers(i), device_id_type=MESH)

    for there, source in sources:

        @pl.when(there)
        def _():
            pl.semaphore_signal(barrier, inc=1, device_id=source, device_id_type=MESH)

    count = 15
    for there in targets:
        count = count + jnp.where(there, 1, 0)
    pl.semaphore_wait(barrier, count)


class Move:
    def __init__(self, source, target, send, recv, where, away):
        self.away, self.home = away, jnp.logical_not(away)
        self.remote = pltpu.make_async_remote_copy(
            source, target, send, recv, device_id=where, device_id_type=MESH
        )
        self.local = pltpu.make_async_copy(source, target, recv)

    def start(self):
        pl.when(self.away)(self.remote.start)
        pl.when(self.home)(self.local.start)

    def wait_recv(self):
        pl.when(self.away)(self.remote.wait_recv)
        pl.when(self.home)(self.local.wait)

    def wait_send(self):
        pl.when(self.away)(self.remote.wait_send)


def advance(centre, north, south, terms, first_lane, last_lane):
    out = []
    for q in range(4):
        mid = centre[q]
        east = pltpu.roll(jnp.where(first_lane, centre[(q + 1) % 4], mid), 127, 1)
        west = pltpu.roll(jnp.where(last_lane, centre[(q + 3) % 4], mid), 1, 1)
        out.append(
            mid
            - ADVECTION * mid * (east - west)
            - terms[4 + q] * (south[q] - north[q])
            + terms[q] * (east + west + north[q] + south[q] - 4.0 * mid)
        )
    return out


def gather_kernel(field, terms, extra, where, out, extra_out, *scratch):
    n = CHUNKS
    low, high, relay, cast, near, far, stage = (scratch[n * k : n * (k + 1)] for k in range(7))
    term_edges, extra_near, where_near, where_far, blocks, once = scratch[7 * n : 7 * n + 6]
    sems = scratch[7 * n + 6 :]
    up_send, down_send, low_recv, high_recv, relay_send, relay_recv = sems[:6]
    spread_send, spread_recv, hop_send, hop_recv, send, recv, table = sems[6:]
    mem, lat = lax.axis_index("mem"), lax.axis_index("lat")
    z, c, h, s, w = place()
    mine = w * 2 + c
    group = m8(z - w + 4 * c)
    patch = group * 2 + c

    def peer(i):
        k = (mine + i) % 16
        return k, device(z, k % 2, h, s, k // 2)

    hops = m8(w - 4 * c) != 0
    hop_to, hop_from = device(m8(w + z - 4 * c), c, h, s, w), device(group, c, h, s, w)
    up_far, down_far = (lat == 15) & (mem != 15), (lat == 16) & (mem != 0)
    up_near, down_near = (lat < 31) & jnp.logical_not(up_far), (lat > 0) & jnp.logical_not(down_far)
    relays_up, relays_down = (lat == mem) & (lat != 15), (lat == mem + 16) & (lat != 16)
    relays = relays_up | relays_down
    low_from = (mem, jnp.where((lat == 16) & (mem != 15), mem, jnp.maximum(lat - 1, 0)))
    high_from = (mem, jnp.where((lat == 15) & (mem != 0), mem + 16, jnp.minimum(lat + 1, 31)))
    relay_from = (mem, jnp.where(relays_up, 15, 16))
    enter(
        lambda i: peer(i)[1],
        ((hops, hop_from), (lat > 0, low_from), (lat < 31, high_from), (relays, relay_from)),
        (hops, lat < 31, lat > 0, relays),
    )

    def remote(source, target, sends, recvs, i, to):
        return pltpu.make_async_remote_copy(
            source, target, sends.at[i], recvs.at[i], device_id=to, device_id_type=MESH
        )

    class Edge:
        def __init__(self, i):
            if i == 0:
                first, last, bottom, top = terms.at[0], terms.at[7], term_edges.at[0], term_edges.at[1]
                held = term_edges.at[2]
            else:
                rows = pl.ds((i - 1) * ROWS, ROWS)
                first, last = field.at[pl.ds(0, 8), rows], field.at[pl.ds(24, 8), rows]
                bottom, top, held = low[i - 1], high[i - 1], relay[i - 1]
            above, below = (mem, jnp.minimum(lat + 1, 31)), (mem, jnp.maximum(lat - 1, 0))
            self.bottom, self.top = bottom, top
            self.ups = (
                (up_near, remote(last, bottom, up_send, low_recv, i, above)),
                (up_far, remote(last, held, up_send, relay_recv, i, (mem, mem))),
            )
            self.downs = (
                (down_near, remote(first, top, down_send, high_recv, i, below)),
                (down_far, remote(first, held, down_send, relay_recv, i, (mem, mem + 16))),
            )
            self.passes = (
                (relays_up, remote(held, bottom, relay_send, low_recv, i, (mem, 16))),
                (relays_down, remote(held, top, relay_send, high_recv, i, (mem, 15))),
            )

        def start(self):
            for there, copy in self.ups + self.downs:
                pl.when(there)(copy.start)

            @pl.when(lat == 0)
            def _():
                self.bottom[...] = jnp.zeros(self.bottom.shape, jnp.float32)

            @pl.when(lat == 31)
            def _():
                self.top[...] = jnp.zeros(self.top.shape, jnp.float32)

        def forward(self):
            for (there, copy), (_, arriving) in zip(self.passes, (self.ups[1], self.downs[1])):

                @pl.when(there)
                def _():
                    arriving.wait_recv()
                    copy.start()

        def wait(self):
            pl.when(lat > 0)(self.ups[0][1].wait_recv)
            pl.when(lat < 31)(self.downs[0][1].wait_recv)

        def end(self):
            for there, copy in self.ups + self.downs + self.passes:
                pl.when(there)(copy.wait_send)

    spread_to = device(z, c, h, s, m8(w - z + 4 * c))
    spreads = m8(4 * c - z) != 0
    parts = list(zip(cast, near, far)) + [(extra, extra_near, extra_out), (where, where_near, where_far)]
    spread = [Move(a, b, spread_send.at[i], spread_recv.at[i], spread_to, spreads) for i, (a, b, _) in enumerate(parts)]
    hop = [Move(b, d, hop_send.at[i], hop_recv.at[i], hop_to, hops) for i, (_, b, d) in enumerate(parts)]

    def piece(i, off):
        k, there = peer(off)
        wanted = m8(z - k // 2 + 4 * (k % 2)) * 2 + k % 2
        return pltpu.make_async_remote_copy(
            stage[i].at[wanted],
            out.at[mine, pl.ds(i * ROWS, ROWS)],
            send.at[i, off],
            recv.at[i, off],
            device_id=there,
            device_id_type=MESH,
        )

    def own(i):
        return pltpu.make_async_copy(stage[i].at[patch], out.at[mine, pl.ds(i * ROWS, ROWS)], recv.at[i, 0])

    lane = lax.broadcasted_iota(jnp.int32, (ROWS, 128), 1)
    first_lane, last_lane = lane == 0, lane == 127

    def forecast(i):
        rows = slice(i * ROWS, (i + 1) * ROWS)

        def before(k):
            if isinstance(k, int) and k < 2:
                return [low[i][4 * k + q] for q in range(4)]
            if isinstance(k, int) and k > 9:
                return [high[i][4 * k - 40 + q] for q in range(4)]
            return [field[4 * k - 8 + q, rows] for q in range(4)]

        def middle(k):
            return [once[4 * k + q] for q in range(4)]

        def first(r):
            if isinstance(r, int) and r == 0:
                own_terms = [term_edges[0, q : q + 1] for q in range(8)]
            elif isinstance(r, int) and r == 9:
                own_terms = [term_edges[1, q : q + 1] for q in range(8)]
            else:
                own_terms = [terms[r - 1, q : q + 1] for q in range(8)]
            new = advance(before(r + 1), before(r), before(r + 2), own_terms, first_lane, last_lane)
            for q in range(4):
                once[4 * r + q] = new[q]

        for r in (0, 1, 8, 9):
            first(r)
        pl.loop(2, 8)(first)

        @pl.loop(0, 8)
        def _(r):
            own_terms = [terms[r, q : q + 1] for q in range(8)]
            new = advance(middle(r + 1), middle(r), middle(r + 2), own_terms, first_lane, last_lane)
            for q in range(4):
                cast[i][4 * r + q] = new[q]

    def observe(i):
        tiles, put = far[i], stage[i]

        @pl.loop(0, 8)
        def _(half):
            for p in range(2):
                for t in range(2):
                    put[2 * half + p, :, t * 128 : (t + 1) * 128] = tiles[4 * half + 2 * p + t]
                for j in range(4):
                    at = half * 8 + p * 4 + j
                    direct = tiles[blocks[0, at]]
                    beside = jnp.where(first_lane, tiles[blocks[1, at]], direct)
                    east = pltpu.roll(beside, 127, 1)
                    flag = extra_out[half, p * 4 + j : p * 4 + j + 1]
                    seen = jnp.where(flag == 1.0, 0.5 * (direct + east), direct)
                    put[2 * half + p, :, 256 + j * 128 : 384 + j * 128] = seen

        @pl.loop(1, 16)
        def _(off):
            piece(i, off).start()

        own(i).start()

    edges = [Edge(i) for i in range(n + 1)]
    for edge in edges:
        edge.start()
    spread[n].start()
    spread[n + 1].start()
    for i, edge in enumerate(edges):
        edge.forward()
        edge.wait()
        if i > 0:
            forecast(i - 1)
            spread[i - 1].start()
        if i == 2:
            for k in (n, n + 1, 0):
                spread[k].wait_recv()
                hop[k].start()
    for i in range(n):
        if i + 1 < n:
            spread[i + 1].wait_recv()
            hop[i + 1].start()
        if i == 0:
            hop[n].wait_recv()
            hop[n + 1].wait_recv()
            read = pltpu.make_async_copy(where_far, blocks, table)
            read.start()
            read.wait()
        hop[i].wait_recv()
        observe(i)
    for edge in edges:
        edge.end()
    for move in spread + hop:
        move.wait_send()
    for i in range(n):

        @pl.loop(1, 16)
        def _(off):
            piece(i, off).wait()

        own(i).wait()


def gather(field, terms, extra, where):
    def buffer(*shape):
        return pltpu.VMEM(shape, jnp.float32)

    n = CHUNKS
    dma, table = pltpu.SemaphoreType.DMA, pltpu.VMEM((8, 128), jnp.int32)
    vmem = pl.BlockSpec(memory_space=pltpu.VMEM)
    return pl.pallas_call(
        gather_kernel,
        out_shape=(
            jax.ShapeDtypeStruct((16, MEMBERS, 768), jnp.float32),
            jax.ShapeDtypeStruct((9, 8, 128), jnp.float32),
        ),
        in_specs=[vmem] * 4,
        out_specs=(vmem, vmem),
        scratch_shapes=[buffer(8, ROWS, 128)] * (3 * n)
        + [buffer(32, ROWS, 128)] * (3 * n)
        + [buffer(16, ROWS, 768)] * n
        + [buffer(3, 8, 128), buffer(9, 8, 128), table, table]
        + [pltpu.SMEM((8, 128), jnp.int32), buffer(40, ROWS, 128)]
        + [dma((n + 1,))] * 6
        + [dma((n + 2,))] * 4
        + [dma((n, 16))] * 2
        + [dma],
        compiler_params=pltpu.CompilerParams(
            collective_id=0, has_side_effects=True, vmem_limit_bytes=40 * 2**20
        ),
        name="gather",
    )(field, terms, extra, where)


def scatter_kernel(cells, out, *scratch):
    held = scratch[:CHUNKS]
    home_send, home_recv, send, recv = scratch[CHUNKS:]
    z, c, h, s, w = place()
    mine = w * 2 + c
    group = m8(z - w + 4 * c)
    patch = group * 2 + c

    def peer(i):
        k = (mine + i) % 16
        return k, device(z, k % 2, h, s, k // 2)

    home, guest = device(group, c, h, s, z), device(w, c, h, s, m8(w - z + 4 * c))
    away = jnp.logical_or(w != z, group != z)
    enter(lambda i: peer(i)[1], ((away, guest),), (away,))

    def piece(i, off):
        k, where = peer(off)
        return pltpu.make_async_remote_copy(
            cells.at[k, pl.ds(i * ROWS, ROWS)],
            held[i].at[patch],
            send.at[i, off],
            recv.at[i, off],
            device_id=where,
            device_id_type=MESH,
        )

    def own(i):
        return pltpu.make_async_copy(cells.at[mine, pl.ds(i * ROWS, ROWS)], held[i].at[patch], recv.at[i, 0])

    def start(i):
        @pl.loop(1, 16)
        def _(off):
            piece(i, off).start()

        own(i).start()

    back = [
        Move(held[i], out.at[:, pl.ds(i * ROWS, ROWS)], home_send.at[i], home_recv.at[i], home, away)
        for i in range(CHUNKS)
    ]
    start(0)
    for i in range(CHUNKS):

        @pl.loop(1, 16)
        def _(off):
            piece(i, off).wait_recv()

        own(i).wait()
        back[i].start()
        if i + 1 < CHUNKS:
            start(i + 1)
    for i in range(CHUNKS):
        back[i].wait_recv()
        back[i].wait_send()

        @pl.loop(1, 16)
        def _(off):
            piece(i, off).wait_send()


def scatter(cells):
    dma = pltpu.SemaphoreType.DMA
    vmem = pl.BlockSpec(memory_space=pltpu.VMEM)
    return pl.pallas_call(
        scatter_kernel,
        out_shape=jax.ShapeDtypeStruct((16, MEMBERS, 256), jnp.float32),
        in_specs=[vmem],
        out_specs=vmem,
        scratch_shapes=[pltpu.VMEM((16, ROWS, 256), jnp.float32)] * CHUNKS
        + [dma((CHUNKS,))] * 2
        + [dma((CHUNKS, 16))] * 2,
        compiler_params=pltpu.CompilerParams(
            collective_id=1, has_side_effects=True, vmem_limit_bytes=40 * 2**20
        ),
        name="scatter",
    )(cells)


def dot(left, right):
    return jnp.dot(left, right, precision=PREC, preferred_element_type=jnp.float32)


def analyse(states, values, errors):
    count = states.shape[0]
    mean = jnp.mean(states, axis=0)
    offset = states - mean
    seen_offset = offset[:, 256:]
    products = lax.dot_general(
        offset, seen_offset, (((0,), (0,)), ((), ())), precision=PREC, preferred_element_type=jnp.float32
    ) / (count - 1.0)
    covariance = products[256:] + jnp.diag(errors)
    scale = lax.rsqrt(jnp.sum(jnp.abs(covariance), axis=1))
    power = jnp.eye(512, dtype=jnp.float32) - covariance * scale[:, None] * scale[None, :]
    gain = products[:256] * scale[None, :]
    for step in range(4):
        gain = gain + dot(gain, power)
        if step < 3:
            power = dot(power, power)
    gain = gain * scale[None, :]
    weights = (values - mean[256:])[None, :] - 0.5 * seen_offset
    update = lax.dot_general(
        weights, gain, (((1,), (1,)), ((), ())), precision=PREC, preferred_element_type=jnp.float32
    )
    return states[:, :256] + update


def body(ensemble, diffusivity, north_wind, observed_blocks, eastern_average_flags, observed_values, observed_error):
    terms = jnp.concatenate([diffusivity.reshape(8, 4, 128), north_wind.reshape(8, 4, 128)], axis=1)
    extra = jnp.concatenate(
        [
            eastern_average_flags[0].astype(jnp.float32).reshape(8, 8, 128),
            jnp.concatenate([observed_values.reshape(1, 4, 128), observed_error.reshape(1, 4, 128)], axis=1),
        ]
    )
    blocks = observed_blocks[0].reshape(1, 64)
    nexts = blocks - blocks % 4 + (blocks + 1) % 4
    where = jnp.pad(jnp.concatenate([blocks, nexts]), ((0, 6), (0, 64)))
    field = ensemble.reshape(MEMBERS, 8, 4, 128).transpose(1, 2, 0, 3).reshape(32, MEMBERS, 128)
    states, extra = gather(field, terms, extra, where)
    states = states.reshape(16 * MEMBERS, 768)
    values, errors = extra[8, :4].reshape(512), extra[8, 4:].reshape(512)
    cells = analyse(states, values, errors).reshape(16, MEMBERS, 256)
    out = scatter(cells)
    return out.reshape(8, 2, MEMBERS, 256).transpose(2, 0, 1, 3).reshape(MEMBERS, 8, 512)


def solution(mesh):
    return jax.shard_map(
        body,
        mesh=mesh,
        in_specs=(
            P("mem", "lat", None),
            P("lat", None),
            P("lat", None),
            P("lat", None, None),
            P("lat", None, None),
            P("lat", "mem", None),
            P("lat", "mem", None),
        ),
        out_specs=P("mem", "lat", None),
        check_vma=False,
    )
```

time: 239 us -> 184 us (0.77)
  the two profiles are of different devices: /device:TPU:419 before, /device:TPU:28 now
where the time goes in v2:
time: 184 us
  Pallas kernels  164 us (89%)
  matrix products  12 us (7%)
  local copies, waits for them, and re-layouts  5.74 us (3%)
  other arithmetic  2.12 us (1%)
    pallas_call x1, Pallas kernels, gather(): pl.pallas_call(gather_kernel, out_shape=(jax.ShapeDtypeStruct((16, MEMBER...  101 us
    pallas_call x1, Pallas kernels, scatter(): pl.pallas_call(scatter_kernel, out_shape=jax.ShapeDtypeStruct((16, MEMBER...  62.7 us
    dot_general x7, matrix products, dot(): jnp.dot(left, right, precision=PREC, preferred_element_type=jnp.float32)  7.85 us

profile of v2, /device:TPU:28, one launch (start us, length us, event | category | flops | bytes accessed | tf_op | source)
XLA Modules:
  0.0 183.7 jit_solution(17796376747447965686)
XLA Ops:
  0.0 0.8 copy.15
  0.8 0.1 reshape_squeeze.7
  0.9 0.7 reshape.173
  1.6 0.7 reshape.174
  2.4 0.8 convert_element_type.10
  3.1 0.7 maximum_maximum_fusion.extra
  3.8 1.8 copy.14
  5.7 101.0 %gather.1 = (f32[16,64,768]{2,1,0:T(8,128)S(1)}, f32[9,8,128]{2,1,0:T(8,128)S(1)}) custom-call(f32[32,64,128]{2,1,0:T(8,128)S(1)} %bitcast.30, f32[8,8,128]{2,1,0:T(8,128)S(1)} %pad_maximum_fusion.terms, f32[9,8,128]{2,1,0:T(8,128)S(1)} %maximum_maximum_fusion.extra, s32[8,128]{1,0:T(8,128)S(1)} %pad.4.where), custom_call_target="tpu_custom_call" | custom-call | tf_op jit(solution)/shard_map/gather/pallas_call | solution.py:301
  106.7 0.2 reduce_sum.18
  106.9 0.2 broadcast_subtract_fusion
  107.1 3.2 %fusion.6 = f32[768,512]{0,1:T(8,128)S(1)} fusion(f32[1024,768]{1,0:T(8,128)S(1)} %broadcast_subtract_fusion), kind=kOutput, calls=%fused_computation.7 | convolution fusion | flops 2416312320 | bytes 6815744 | tf_op jit(solution)/shard_map/dot_general | solution.py:413
  110.3 0.2 abs_reduce_fusion
  110.5 0.7 convolution_add_fusion.3
  111.2 2.1 %fusion.15 = f32[512,512]{1,0:T(8,128)S(1)} fusion(f32[768,512]{0,1:T(8,128)S(1)} %fusion.6, f32[512]{0:T(512)S(1)} %rsqrt.11, f32[512]{0:T(512)S(1)} %slice_bitcast_fusion), kind=kOutput, calls=%fused_computation.20 | convolution fusion | flops 807141376 | bytes 2103296 | tf_op jit(solution)/shard_map/dot_general | solution.py:405
  113.3 1.0 convolution_add_fusion.2
  114.3 1.0 fusion.32
  115.4 1.0 convolution_add_fusion.1
  116.4 1.0 fusion.33
  117.4 1.0 fusion.12
  118.4 1.0 fusion.9
  119.4 62.7 %scatter.1 = f32[16,64,256]{2,1,0:T(8,128)S(1)} custom-call(f32[16,64,256]{2,1,0:T(8,128)S(1)} %bitcast.32), custom_call_target="tpu_custom_call" | custom-call | tf_op jit(solution)/shard_map/scatter/pallas_call | solution.py:389
  182.2 1.6 copy.19
  (9 shorter events, 0.1 us)

commit v3 on v2

v3 whole, which is shorter than its diff:
```python
import jax
import jax.numpy as jnp
from jax import lax
from jax.experimental import pallas as pl
from jax.experimental.pallas import tpu as pltpu
from jax.sharding import PartitionSpec as P

MESH = pl.DeviceIdType.MESH
ADVECTION = 0.1
MEMBERS = 64
OUT = (16, 16, 16, 16)
BACK = (16, 16, 16, 16)
PREC = lax.Precision.HIGH

PEERS = (
    (0, 1, 0), (1, 0, 0), (3, 0, 0), (2, 1, 0), (1, 1, 0), (3, 1, 0), (2, 0, 0), (0, 1, 1),
    (1, 0, 1), (3, 0, 1), (2, 1, 1), (0, 0, 1), (1, 1, 1), (3, 1, 1), (2, 0, 1),
)

SPIN, SIDE = (7, 3, 5), 5


def both(*values):
    return sum(sum(v // 2**i % 2 for v in values) % 2 * 2**i for i in range(3))


def mix(rows, v):
    return sum(sum(v // 2**j % 2 for j in range(3) if rows[i] // 2**j % 2) % 2 * 2**i for i in range(3))


UNSPIN = next(
    rows
    for rows in ((i, j, k) for i in range(8) for j in range(8) for k in range(8))
    if all(mix(rows, mix(SPIN, v)) == v for v in range(8))
)


def lane(w, z, c):
    return both(w, mix(SPIN, z), SIDE * c)


def member(z, w, c):
    return mix(UNSPIN, both(z, w, SIDE * c))


def device(z, c, h, s, w):
    return (z * 2 + c, h * 16 + (w // 2) * 4 + s * 2 + w % 2)


def place():
    m, l = lax.axis_index("mem"), lax.axis_index("lat")
    return m // 2, m % 2, l // 16, (l % 4) // 2, ((l // 4) % 4) * 2 + l % 2


def enter(peers, sources, targets):
    barrier = pltpu.get_barrier_semaphore()

    for i in range(1, 16):
        pl.semaphore_signal(barrier, inc=1, device_id=peers(i), device_id_type=MESH)

    for there, source in sources:

        @pl.when(there)
        def _():
            pl.semaphore_signal(barrier, inc=1, device_id=source, device_id_type=MESH)

    count = 15
    for there in targets:
        count = count + jnp.where(there, 1, 0)
    pl.semaphore_wait(barrier, count)


def rows(sizes, i):
    return pl.ds(sum(sizes[:i]), sizes[i])


class Move:
    def __init__(self, source, target, send, recv, where, away):
        self.away, self.home = away, jnp.logical_not(away)
        self.remote = pltpu.make_async_remote_copy(
            source, target, send, recv, device_id=where, device_id_type=MESH
        )
        self.local = pltpu.make_async_copy(source, target, recv)

    def start(self):
        pl.when(self.away)(self.remote.start)
        pl.when(self.home)(self.local.start)

    def wait_recv(self):
        pl.when(self.away)(self.remote.wait_recv)
        pl.when(self.home)(self.local.wait)

    def wait_send(self):
        pl.when(self.away)(self.remote.wait_send)


def advance(centre, north, south, terms, first_lane, last_lane):
    out = []
    for q in range(4):
        mid = centre[q]
        east = pltpu.roll(jnp.where(first_lane, centre[(q + 1) % 4], mid), 127, 1)
        west = pltpu.roll(jnp.where(last_lane, centre[(q + 3) % 4], mid), 1, 1)
        out.append(
            mid
            - ADVECTION * mid * (east - west)
            - terms[4 + q] * (south[q] - north[q])
            + terms[q] * (east + west + north[q] + south[q] - 4.0 * mid)
        )
    return out


def gather_kernel(field, diffusivity, north_wind, flags, values, errors, where, out, *rest):
    n = len(OUT)
    values_out, errors_out, *scratch = rest
    low, high, relay, cast, near, far, stage = (scratch[n * k : n * (k + 1)] for k in range(7))
    diffusivity_edges, wind_edges, values_near, errors_near, flags_near, flags_far = scratch[7 * n : 7 * n + 6]
    where_near, where_far, blocks, once, factors, averaged, *sems = scratch[7 * n + 6 :]
    up_send, down_send, low_recv, high_recv, relay_send, relay_recv = sems[:6]
    spread_send, spread_recv, hop_send, hop_recv, send, recv, table = sems[6:]
    mem, lat = lax.axis_index("mem"), lax.axis_index("lat")
    z, c, h, s, w = place()
    mine = w * 2 + c
    group = member(z, w, c)
    patch = group * 2 + c

    def peer(i):
        dx, dy, dc = PEERS[i - 1]
        k = ((w // 2 + dx) % 4) * 4 + ((w + dy) % 2) * 2 + (c + dc) % 2
        return k, device(z, k % 2, h, s, k // 2)

    hops = lane(w, z, c) != z
    hop_to, hop_from = device(lane(w, z, c), c, h, s, w), device(group, c, h, s, w)
    up_far, down_far = (lat == 15) & (mem != 15), (lat == 16) & (mem != 0)
    up_near, down_near = (lat < 31) & jnp.logical_not(up_far), (lat > 0) & jnp.logical_not(down_far)
    relays_up, relays_down = (lat == mem) & (lat != 15), (lat == mem + 16) & (lat != 16)
    relays = relays_up | relays_down
    low_from = (mem, jnp.where((lat == 16) & (mem != 15), mem, jnp.maximum(lat - 1, 0)))
    high_from = (mem, jnp.where((lat == 15) & (mem != 0), mem + 16, jnp.minimum(lat + 1, 31)))
    relay_from = (mem, jnp.where(relays_up, 15, 16))
    enter(
        lambda i: peer(i)[1],
        ((hops, hop_from), (lat > 0, low_from), (lat < 31, high_from), (relays, relay_from)),
        (hops, lat < 31, lat > 0, relays),
    )

    def remote(source, target, sends, recvs, i, to):
        return pltpu.make_async_remote_copy(
            source, target, sends.at[i], recvs.at[i], device_id=to, device_id_type=MESH
        )

    class Edge:
        def __init__(self, i):
            if i < 2:
                ref, ends = ((diffusivity, diffusivity_edges), (north_wind, wind_edges))[i]
                first, last = ref.at[pl.ds(0, 1)], ref.at[pl.ds(7, 1)]
                bottom, top, held = ends.at[0], ends.at[1], ends.at[2]
            else:
                part = rows(OUT, i - 2)
                first, last = field.at[pl.ds(0, 8), part], field.at[pl.ds(24, 8), part]
                bottom, top, held = low[i - 2], high[i - 2], relay[i - 2]
            above, below = (mem, jnp.minimum(lat + 1, 31)), (mem, jnp.maximum(lat - 1, 0))
            self.bottom, self.top = bottom, top
            self.ups = (
                (up_near, remote(last, bottom, up_send, low_recv, i, above)),
                (up_far, remote(last, held, up_send, relay_recv, i, (mem, mem))),
            )
            self.downs = (
                (down_near, remote(first, top, down_send, high_recv, i, below)),
                (down_far, remote(first, held, down_send, relay_recv, i, (mem, mem + 16))),
            )
            self.passes = (
                (relays_up, remote(held, bottom, relay_send, low_recv, i, (mem, 16))),
                (relays_down, remote(held, top, relay_send, high_recv, i, (mem, 15))),
            )

        def start(self, far):
            for there, copy in (self.ups[far], self.downs[far]):
                pl.when(there)(copy.start)

        def fill(self):
            @pl.when(lat == 0)
            def _():
                self.bottom[...] = jnp.zeros(self.bottom.shape, jnp.float32)

            @pl.when(lat == 31)
            def _():
                self.top[...] = jnp.zeros(self.top.shape, jnp.float32)

        def forward(self):
            for (there, copy), (_, arriving) in zip(self.passes, (self.ups[1], self.downs[1])):

                @pl.when(there)
                def _():
                    arriving.wait_recv()
                    copy.start()

        def wait(self):
            pl.when(lat > 0)(self.ups[0][1].wait_recv)
            pl.when(lat < 31)(self.downs[0][1].wait_recv)

        def end(self):
            for there, copy in self.ups + self.downs + self.passes:
                pl.when(there)(copy.wait_send)

    spread_to = device(z, c, h, s, lane(w, z, c))
    spreads = lane(w, z, c) != w
    parts = list(zip(cast, near, far)) + [
        (flags, flags_near, flags_far),
        (where, where_near, where_far),
        (values, values_near, values_out),
        (errors, errors_near, errors_out),
    ]
    spread = [Move(a, b, spread_send.at[i], spread_recv.at[i], spread_to, spreads) for i, (a, b, _) in enumerate(parts)]
    hop = [Move(b, d, hop_send.at[i], hop_recv.at[i], hop_to, hops) for i, (_, b, d) in enumerate(parts)]

    def piece(i, off):
        k, there = peer(off)
        wanted = member(z, k // 2, k % 2) * 2 + k % 2
        return pltpu.make_async_remote_copy(
            stage[i].at[wanted],
            out.at[mine, rows(OUT, i)],
            send.at[i, off],
            recv.at[i, off],
            device_id=there,
            device_id_type=MESH,
        )

    def own(i):
        return pltpu.make_async_copy(stage[i].at[patch], out.at[mine, rows(OUT, i)], recv.at[i, 0])

    def ends(i):
        column = lax.broadcasted_iota(jnp.int32, (OUT[i], 128), 1)
        return column == 0, column == 127

    def tile(k):
        return [factors[k, q : q + 1] for q in range(8)]

    def forecast(i):
        size, part = OUT[i], rows(OUT, i)
        first_lane, last_lane = ends(i)

        def before(k):
            if isinstance(k, int) and k < 2:
                return [low[i][4 * k + q] for q in range(4)]
            if isinstance(k, int) and k > 9:
                return [high[i][4 * k - 40 + q] for q in range(4)]
            return [field[4 * k - 8 + q, part] for q in range(4)]

        def middle(k):
            return [once[4 * k + q, :size] for q in range(4)]

        def first(r):
            new = advance(before(r + 1), before(r), before(r + 2), tile(r), first_lane, last_lane)
            for q in range(4):
                once[4 * r + q, :size] = new[q]

        for r in (0, 1, 8, 9):
            first(r)
        pl.loop(2, 8)(first)

        @pl.loop(0, 8)
        def _(r):
            new = advance(middle(r + 1), middle(r), middle(r + 2), tile(r + 1), first_lane, last_lane)
            for q in range(4):
                cast[i][4 * r + q] = new[q]

    def observe(i):
        tiles, put = far[i], stage[i]
        first_lane, _ = ends(i)

        @pl.loop(0, 8)
        def _(half):
            for p in range(2):
                for t in range(2):
                    put[2 * half + p, :, t * 128 : (t + 1) * 128] = tiles[4 * half + 2 * p + t]
                for j in range(4):
                    at = half * 8 + p * 4 + j
                    direct = tiles[blocks[0, at]]
                    beside = jnp.where(first_lane, tiles[blocks[1, at]], direct)
                    east = pltpu.roll(beside, 127, 1)
                    flag = averaged[half, p * 4 + j : p * 4 + j + 1]
                    seen = jnp.where(flag == 1, 0.5 * (direct + east), direct)
                    put[2 * half + p, :, 256 + j * 128 : 384 + j * 128] = seen

        for off in range(1, 16):
            piece(i, off).start()

        own(i).start()

    edges = [Edge(i) for i in range(n + 2)]
    for edge in edges:
        edge.start(1)
    for edge in edges:
        edge.start(0)
    for edge in edges:
        edge.fill()
    for edge in edges:
        edge.forward()
    for move in spread[n:]:
        move.start()
    for k, ref in enumerate((diffusivity, north_wind)):
        for q in range(4):
            for r in range(8):
                factors[r + 1, 4 * k + q : 4 * k + q + 1] = ref[r : r + 1, q * 128 : (q + 1) * 128]
    for k, ref in enumerate((diffusivity_edges, wind_edges)):
        edges[k].wait()
        for q in range(4):
            for at, r in ((0, 0), (1, 9)):
                factors[r, 4 * k + q : 4 * k + q + 1] = ref[at, :, q * 128 : (q + 1) * 128]
    for i in range(n):
        edges[i + 2].wait()
        forecast(i)
        spread[i].start()
        if i == 1:
            for move, after in zip(spread[n:] + spread[:1], hop[n:] + hop[:1]):
                move.wait_recv()
                after.start()
    for i in range(n):
        if i + 1 < n:
            spread[i + 1].wait_recv()
            hop[i + 1].start()
        if i == 0:
            for move in hop[n:]:
                move.wait_recv()
            for p in range(16):
                for j in range(4):
                    at = p % 2 * 4 + j
                    averaged[p // 2, at : at + 1] = flags_far[p : p + 1, j * 128 : (j + 1) * 128]
            read = pltpu.make_async_copy(where_far, blocks, table)
            read.start()
            read.wait()
        hop[i].wait_recv()
        observe(i)
    for edge in edges:
        edge.end()
    for move in spread + hop:
        move.wait_send()
    for i in range(n):

        for off in range(1, 16):
            piece(i, off).wait()

        own(i).wait()


def gather(field, diffusivity, north_wind, flags, values, errors, where):
    def buffer(*shape, dtype=jnp.float32):
        return pltpu.VMEM(shape, dtype)

    n = len(OUT)
    dma, table = pltpu.SemaphoreType.DMA, buffer(8, 128, dtype=jnp.int32)
    vmem = pl.BlockSpec(memory_space=pltpu.VMEM)
    row = jax.ShapeDtypeStruct((1, 512), jnp.float32)
    return pl.pallas_call(
        gather_kernel,
        out_shape=(jax.ShapeDtypeStruct((16, MEMBERS, 768), jnp.float32), row, row),
        in_specs=[vmem] * 7,
        out_specs=(vmem,) * 3,
        scratch_shapes=[buffer(8, size, 128) for size in OUT * 3]
        + [buffer(32, size, 128) for size in OUT * 3]
        + [buffer(16, size, 768) for size in OUT]
        + [buffer(3, 1, 512)] * 2
        + [buffer(1, 512)] * 2
        + [buffer(16, 512, dtype=jnp.int32)] * 2
        + [table, table, pltpu.SMEM((8, 128), jnp.int32), buffer(40, max(OUT), 128)]
        + [buffer(10, 8, 128), buffer(8, 8, 128, dtype=jnp.int32)]
        + [dma((n + 2,))] * 6
        + [dma((n + 4,))] * 4
        + [dma((n, 16))] * 2
        + [dma],
        compiler_params=pltpu.CompilerParams(
            collective_id=0, has_side_effects=True, vmem_limit_bytes=40 * 2**20
        ),
        name="gather",
    )(field, diffusivity, north_wind, flags, values, errors, where)


def scatter_kernel(cells, out, *scratch):
    held = scratch[:len(BACK)]
    home_send, home_recv, send, recv = scratch[len(BACK):]
    z, c, h, s, w = place()
    mine = w * 2 + c
    group = member(z, w, c)
    patch = group * 2 + c

    def peer(i):
        dx, dy, dc = PEERS[i - 1]
        k = ((w // 2 + dx) % 4) * 4 + ((w + dy) % 2) * 2 + (c + dc) % 2
        return k, device(z, k % 2, h, s, k // 2)

    home, guest = device(group, c, h, s, z), device(w, c, h, s, lane(w, z, c))
    away = jnp.logical_or(w != z, group != z)
    enter(lambda i: peer(i)[1], ((away, guest),), (away,))

    def piece(i, off):
        k, where = peer(off)
        return pltpu.make_async_remote_copy(
            cells.at[k, rows(BACK, i)],
            held[i].at[patch],
            send.at[i, off],
            recv.at[i, off],
            device_id=where,
            device_id_type=MESH,
        )

    def own(i):
        return pltpu.make_async_copy(cells.at[mine, rows(BACK, i)], held[i].at[patch], recv.at[i, 0])

    def start(i):
        for off in range(1, 16):
            piece(i, off).start()

        own(i).start()

    back = [
        Move(held[i], out.at[:, rows(BACK, i)], home_send.at[i], home_recv.at[i], home, away)
        for i in range(len(BACK))
    ]
    start(0)
    for i in range(len(BACK)):

        for off in range(1, 16):
            piece(i, off).wait_recv()

        own(i).wait()
        back[i].start()
        if i + 1 < len(BACK):
            start(i + 1)
    for i in range(len(BACK)):
        back[i].wait_recv()
        back[i].wait_send()

        for off in range(1, 16):
            piece(i, off).wait_send()


def scatter(cells):
    dma = pltpu.SemaphoreType.DMA
    vmem = pl.BlockSpec(memory_space=pltpu.VMEM)
    return pl.pallas_call(
        scatter_kernel,
        out_shape=jax.ShapeDtypeStruct((16, MEMBERS, 256), jnp.float32),
        in_specs=[vmem],
        out_specs=vmem,
        scratch_shapes=[pltpu.VMEM((16, size, 256), jnp.float32) for size in BACK]
        + [dma((len(BACK),))] * 2
        + [dma((len(BACK), 16))] * 2,
        compiler_params=pltpu.CompilerParams(
            collective_id=1, has_side_effects=True, vmem_limit_bytes=40 * 2**20
        ),
        name="scatter",
    )(cells)


def dot(left, right):
    return jnp.dot(left, right, precision=PREC, preferred_element_type=jnp.float32)


def analyse(states, values, errors):
    count = states.shape[0]
    mean = jnp.mean(states, axis=0)
    offset = states - mean
    seen_offset = offset[:, 256:]
    products = lax.dot_general(
        offset, seen_offset, (((0,), (0,)), ((), ())), precision=PREC, preferred_element_type=jnp.float32
    ) / (count - 1.0)
    covariance = products[256:] + jnp.diag(errors)
    scale = lax.rsqrt(jnp.sum(jnp.abs(covariance), axis=1))
    power = jnp.eye(512, dtype=jnp.float32) - covariance * scale[:, None] * scale[None, :]
    gain = products[:256] * scale[None, :]
    for step in range(4):
        gain = gain + dot(gain, power)
        if step < 3:
            power = dot(power, power)
    gain = gain * scale[None, :]
    weights = (values - mean[256:])[None, :] - 0.5 * seen_offset
    update = lax.dot_general(
        weights, gain, (((1,), (1,)), ((), ())), precision=PREC, preferred_element_type=jnp.float32
    )
    return states[:, :256] + update


def body(ensemble, diffusivity, north_wind, observed_blocks, eastern_average_flags, observed_values, observed_error):
    blocks = observed_blocks[0].reshape(1, 64)
    nexts = blocks - blocks % 4 + (blocks + 1) % 4
    where = jnp.pad(jnp.concatenate([blocks, nexts]), ((0, 6), (0, 64)))
    field = ensemble.reshape(MEMBERS, 8, 4, 128).transpose(1, 2, 0, 3).reshape(32, MEMBERS, 128)
    states, values, errors = gather(
        field, diffusivity, north_wind, eastern_average_flags[0], observed_values[0], observed_error[0], where
    )
    states, values, errors = states.reshape(16 * MEMBERS, 768), values[0], errors[0]
    cells = analyse(states, values, errors).reshape(16, MEMBERS, 256)
    out = scatter(cells)
    return out.reshape(8, 2, MEMBERS, 256).transpose(2, 0, 1, 3).reshape(MEMBERS, 8, 512)


def solution(mesh):
    return jax.shard_map(
        body,
        mesh=mesh,
        in_specs=(
            P("mem", "lat", None),
            P("lat", None),
            P("lat", None),
            P("lat", None, None),
            P("lat", None, None),
            P("lat", "mem", None),
            P("lat", "mem", None),
        ),
        out_specs=P("mem", "lat", None),
        check_vma=False,
    )
```

time: 184 us -> 168 us (0.913)
  the two profiles are of different devices: /device:TPU:28 before, /device:TPU:21 now
where the time goes in v3:
time: 168 us
  Pallas kernels  150 us (89%)
  matrix products  12.3 us (7%)
  local copies, waits for them, and re-layouts  4.34 us (3%)
    pallas_call x1, Pallas kernels, gather(): pl.pallas_call(gather_kernel, out_shape=(jax.ShapeDtypeStruct((16, MEMBER...  84.8 us
    pallas_call x1, Pallas kernels, scatter(): pl.pallas_call(scatter_kernel, out_shape=jax.ShapeDtypeStruct((16, MEMBER...  65.5 us
    dot_general x7, matrix products, dot(): jnp.dot(left, right, precision=PREC, preferred_element_type=jnp.float32)  7.85 us

profile of v3, /device:TPU:21, one launch (start us, length us, event | category | flops | bytes accessed | tf_op | source)
XLA Modules:
  0.0 167.7 jit_solution(6832309792556398392)
XLA Ops:
  0.0 0.0 copy-start.4
  0.0 0.0 copy-start.3
  0.0 0.0 copy-start
  0.0 0.0 copy-start.2
  0.0 0.0 copy-start.1
  0.0 0.8 copy.15
  0.8 0.1 reshape_squeeze.3
  1.0 1.8 %copy.14 = f32[64,8,4,128]{3,0,2,1:T(8,128)S(1)} copy(f32[64,8,4,128]{3,1,2,0:T(8,128)} %bitcast.39) | data formatting | bytes 2097152 | tf_op jit(solution)/shard_map/reshape | solution.py:487
  2.8 0.0 copy-done.4
  2.8 0.0 copy-done.3
  2.8 0.0 copy-done
  2.8 0.0 copy-done.2
  2.9 0.0 copy-done.1
  2.9 84.8 %gather.1 = (f32[16,64,768]{2,1,0:T(8,128)S(1)}, f32[1,512]{1,0:T(1,128)S(1)}, f32[1,512]{1,0:T(1,128)S(1)}) custom-call(f32[32,64,128]{2,1,0:T(8,128)S(1)} %bitcast.29, f32[8,512]{1,0:T(8,128)S(1)} %copy-done.1, f32[8,512]{1,0:T(8,128)S(1)} %copy-done.2, s32[16,512]{1,0:T(8,128)S(1)} %bitcast.32, f32[1,512]{1,0:T(1,128)S(1)} %bitcast.33, ...), custom_call_target="tpu_custom_call" | custom-call | tf_op jit(solution)/shard_map/gather/pallas_call | solution.py:354
  87.6 0.2 reduce_sum.18
  87.9 0.2 broadcast_subtract_fusion
  88.1 3.2 %fusion.6 = f32[768,512]{0,1:T(8,128)S(1)} fusion(f32[1024,768]{1,0:T(8,128)S(1)} %broadcast_subtract_fusion), kind=kOutput, calls=%fused_computation.7 | convolution fusion | flops 2416312320 | bytes 6815744 | tf_op jit(solution)/shard_map/dot_general | solution.py:464
  91.3 0.2 abs_reduce_fusion
  91.4 0.7 convolution_add_fusion.3
  92.2 2.1 %fusion.15 = f32[512,512]{1,0:T(8,128)S(1)} fusion(f32[768,512]{0,1:T(8,128)S(1)} %fusion.6, f32[512]{0:T(512)S(1)} %rsqrt.11, f32[512]{0:T(512)S(1)} %bitcast.37), kind=kOutput, calls=%fused_computation.20 | convolution fusion | flops 807141376 | bytes 2103296 | tf_op jit(solution)/shard_map/dot_general | solution.py:456
  94.3 1.0 convolution_add_fusion.2
  95.3 1.0 fusion.32
  96.3 1.0 convolution_add_fusion.1
  97.3 1.0 fusion.33
  98.3 1.0 fusion.12
  99.3 1.3 fusion.9
  100.6 65.5 %scatter.1 = f32[16,64,256]{2,1,0:T(8,128)S(1)} custom-call(f32[16,64,256]{2,1,0:T(8,128)S(1)} %bitcast.31), custom_call_target="tpu_custom_call" | custom-call | tf_op jit(solution)/shard_map/scatter/pallas_call | solution.py:440
  166.1 1.6 copy.19
  (6 shorter events, 0.0 us)
Async XLA Ops:
  0.0 2.8 %copy-start.4 = (f32[1,1,512]{2,1,0:T(1,128)S(1)}, f32[1,1,512]{2,1,0:T(1,128)}, u32[]{:S(2)}) copy-start(f32[1,1,512]{2,1,0:T(1,128)} %param.13) | copy-start | bytes 6148
  0.0 2.8 %copy-start.3 = (f32[1,1,512]{2,1,0:T(1,128)S(1)}, f32[1,1,512]{2,1,0:T(1,128)}, u32[]{:S(2)}) copy-start(f32[1,1,512]{2,1,0:T(1,128)} %param.12) | copy-start | bytes 6148
  0.0 2.8 %copy-start = (s32[1,16,512]{2,1,0:T(8,128)S(1)}, s32[1,16,512]{2,1,0:T(8,128)}, u32[]{:S(2)}) copy-start(s32[1,16,512]{2,1,0:T(8,128)} %param.11) | copy-start | bytes 98308
  0.0 2.8 %copy-start.2 = (f32[8,512]{1,0:T(8,128)S(1)}, f32[8,512]{1,0:T(8,128)}, u32[]{:S(2)}) copy-start(f32[8,512]{1,0:T(8,128)} %north_wind.1) | copy-start | bytes 49156
  0.0 2.8 %copy-start.1 = (f32[8,512]{1,0:T(8,128)S(1)}, f32[8,512]{1,0:T(8,128)}, u32[]{:S(2)}) copy-start(f32[8,512]{1,0:T(8,128)} %diffusivity.1) | copy-start | bytes 49156

commit v4 on v3

--- a/solution.py
+++ b/solution.py
@@ -290,12 +290,14 @@
     edges = [Edge(i) for i in range(n + 2)]
     for edge in edges:
         edge.start(1)
-    for edge in edges:
+    for edge in edges[:3]:
         edge.start(0)
     for edge in edges:
         edge.fill()
     for edge in edges:
         edge.forward()
+    for edge in edges[3:]:
+        edge.start(0)
     for move in spread[n:]:
         move.start()
     for k, ref in enumerate((diffusivity, north_wind)):
@@ -468,11 +470,10 @@
     scale = lax.rsqrt(jnp.sum(jnp.abs(covariance), axis=1))
     power = jnp.eye(512, dtype=jnp.float32) - covariance * scale[:, None] * scale[None, :]
     gain = products[:256] * scale[None, :]
-    for step in range(4):
-        gain = gain + dot(gain, power)
-        if step < 3:
-            power = dot(power, power)
-    gain = gain * scale[None, :]
+    for _ in range(3):
+        both_products = dot(jnp.concatenate([gain, power]), power)
+        gain, power = gain + both_products[:256], both_products[256:]
+    gain = (gain + dot(gain, power)) * scale[None, :]
     weights = (values - mean[256:])[None, :] - 0.5 * seen_offset
     update = lax.dot_general(
         weights, gain, (((1,), (1,)), ((), ())), precision=PREC, preferred_element_type=jnp.float32

time: 168 us -> 165 us (0.982)
  matrix products: 12.3 us -> 8.85 us
    dot_general x7 -> x4, matrix products: 7.85 us -> 5.08 us  [dot(): jnp.dot(left, right, precision=PREC, preferred_element_type=jnp.float32)]
where the time goes in v4:
time: 165 us
  Pallas kernels  150 us (91%)
  matrix products  8.85 us (5%)
  local copies, waits for them, and re-layouts  4.48 us (3%)
    pallas_call x1, Pallas kernels, gather(): pl.pallas_call(gather_kernel, out_shape=(jax.ShapeDtypeStruct((16, MEMBER...  84.7 us
    pallas_call x1, Pallas kernels, scatter(): pl.pallas_call(scatter_kernel, out_shape=jax.ShapeDtypeStruct((16, MEMBER...  65.5 us
    dot_general x4, matrix products, dot(): jnp.dot(left, right, precision=PREC, preferred_element_type=jnp.float32)  5.08 us

profile of v4, /device:TPU:21, one launch (start us, length us, event | category | flops | bytes accessed | tf_op | source)
XLA Modules:
  0.0 165.0 jit_solution(4707487025999997411)
XLA Ops:
  0.0 0.0 copy-start.4
  0.0 0.0 copy-start.3
  0.0 0.0 copy-start
  0.0 0.0 copy-start.2
  0.0 0.0 copy-start.1
  0.0 0.8 copy.12
  0.8 0.1 reshape_squeeze.3
  1.0 1.8 %copy.11 = f32[64,8,4,128]{3,0,2,1:T(8,128)S(1)} copy(f32[64,8,4,128]{3,1,2,0:T(8,128)} %bitcast.31) | data formatting | bytes 2097152 | tf_op jit(solution)/shard_map/reshape | solution.py:488
  2.8 0.0 copy-done.4
  2.8 0.0 copy-done.3
  2.8 0.0 copy-done
  2.8 0.0 copy-done.2
  2.9 0.0 copy-done.1
  2.9 84.7 %gather.1 = (f32[16,64,768]{2,1,0:T(8,128)S(1)}, f32[1,512]{1,0:T(1,128)S(1)}, f32[1,512]{1,0:T(1,128)S(1)}) custom-call(f32[32,64,128]{2,1,0:T(8,128)S(1)} %bitcast.22, f32[8,512]{1,0:T(8,128)S(1)} %copy-done.1, f32[8,512]{1,0:T(8,128)S(1)} %copy-done.2, s32[16,512]{1,0:T(8,128)S(1)} %bitcast.25, f32[1,512]{1,0:T(1,128)S(1)} %bitcast.28, ...), custom_call_target="tpu_custom_call" | custom-call | tf_op jit(solution)/shard_map/gather/pallas_call | solution.py:356
  87.5 0.2 reduce_sum.18
  87.8 0.2 broadcast_subtract_fusion
  88.0 2.7 %fusion.18 = f32[768,512]{1,0:T(8,128)S(1)} fusion(f32[1024,768]{1,0:T(8,128)S(1)} %broadcast_subtract_fusion), kind=kOutput, calls=%fused_computation.19 | convolution fusion | flops 2416312320 | bytes 6815744 | tf_op jit(solution)/shard_map/dot_general | solution.py:466
  90.7 0.3 abs_reduce_fusion
  91.0 0.1 slice_multiply_fusion
  91.1 0.2 multiply_subtract_fusion
  91.3 1.5 fusion.6
  92.8 0.1 slice_add_fusion.4
  92.9 0.1 slice.49
  93.0 1.5 fusion.10
  94.4 0.1 slice_add_fusion.3
  94.5 0.1 slice.51
  94.6 1.5 fusion.14
  96.1 0.7 fusion.24
  96.8 1.1 fusion.21
  97.9 65.5 %scatter.1 = f32[16,64,256]{2,1,0:T(8,128)S(1)} custom-call(f32[16,64,256]{2,1,0:T(8,128)S(1)} %bitcast.24), custom_call_target="tpu_custom_call" | custom-call | tf_op jit(solution)/shard_map/scatter/pallas_call | solution.py:442
  163.4 1.6 copy.13
  (6 shorter events, 0.0 us)
Async XLA Ops:
  0.0 2.8 %copy-start.4 = (f32[1,1,512]{2,1,0:T(1,128)S(1)}, f32[1,1,512]{2,1,0:T(1,128)}, u32[]{:S(2)}) copy-start(f32[1,1,512]{2,1,0:T(1,128)} %param.13) | copy-start | bytes 6148
  0.0 2.8 %copy-start.3 = (f32[1,1,512]{2,1,0:T(1,128)S(1)}, f32[1,1,512]{2,1,0:T(1,128)}, u32[]{:S(2)}) copy-start(f32[1,1,512]{2,1,0:T(1,128)} %param.12) | copy-start | bytes 6148
  0.0 2.8 %copy-start = (s32[1,16,512]{2,1,0:T(8,128)S(1)}, s32[1,16,512]{2,1,0:T(8,128)}, u32[]{:S(2)}) copy-start(s32[1,16,512]{2,1,0:T(8,128)} %param.11) | copy-start | bytes 98308
  0.0 2.8 %copy-start.2 = (f32[8,512]{1,0:T(8,128)S(1)}, f32[8,512]{1,0:T(8,128)}, u32[]{:S(2)}) copy-start(f32[8,512]{1,0:T(8,128)} %north_wind.1) | copy-start | bytes 49156
  0.0 2.8 %copy-start.1 = (f32[8,512]{1,0:T(8,128)S(1)}, f32[8,512]{1,0:T(8,128)}, u32[]{:S(2)}) copy-start(f32[8,512]{1,0:T(8,128)} %diffusivity.1) | copy-start | bytes 49156

commit v5 on v4

--- a/solution.py
+++ b/solution.py
@@ -8,7 +8,7 @@
 MESH = pl.DeviceIdType.MESH
 ADVECTION = 0.1
 MEMBERS = 64
-OUT = (16, 16, 16, 16)
+OUT = (8, 16, 16, 16, 8)
 BACK = (16, 16, 16, 16)
 PREC = lax.Precision.HIGH
 

time: 165 us -> 165 us (level)
    pallas_call x1, Pallas kernels: 65.5 us -> 67.9 us  [scatter(): pl.pallas_call(scatter_kernel, out_shape=jax.ShapeDtypeStruct((16, MEMBER...]
    pallas_call x1, Pallas kernels: 84.7 us -> 82.5 us  [gather(): pl.pallas_call(gather_kernel, out_shape=(jax.ShapeDtypeStruct((16, MEMBER...]
where the time goes in v5:
time: 165 us
  Pallas kernels  150 us (91%)
  matrix products  8.87 us (5%)
  local copies, waits for them, and re-layouts  4.48 us (3%)
    pallas_call x1, Pallas kernels, gather(): pl.pallas_call(gather_kernel, out_shape=(jax.ShapeDtypeStruct((16, MEMBER...  82.5 us
    pallas_call x1, Pallas kernels, scatter(): pl.pallas_call(scatter_kernel, out_shape=jax.ShapeDtypeStruct((16, MEMBER...  67.9 us
    dot_general x4, matrix products, dot(): jnp.dot(left, right, precision=PREC, preferred_element_type=jnp.float32)  5.1 us

profile of v5, /device:TPU:21, one launch (start us, length us, event | category | flops | bytes accessed | tf_op | source)
XLA Modules:
  0.0 165.1 jit_solution(12880737290939021027)
XLA Ops:
  0.0 0.0 copy-start.4
  0.0 0.0 copy-start.3
  0.0 0.0 copy-start
  0.0 0.0 copy-start.2
  0.0 0.0 copy-start.1
  0.0 0.8 copy.12
  0.8 0.1 reshape_squeeze.3
  1.0 1.8 %copy.11 = f32[64,8,4,128]{3,0,2,1:T(8,128)S(1)} copy(f32[64,8,4,128]{3,1,2,0:T(8,128)} %bitcast.31) | data formatting | bytes 2097152 | tf_op jit(solution)/shard_map/reshape | solution.py:488
  2.8 0.0 copy-done.4
  2.8 0.0 copy-done.3
  2.8 0.0 copy-done
  2.8 0.0 copy-done.2
  2.9 0.0 copy-done.1
  2.9 82.5 %gather.1 = (f32[16,64,768]{2,1,0:T(8,128)S(1)}, f32[1,512]{1,0:T(1,128)S(1)}, f32[1,512]{1,0:T(1,128)S(1)}) custom-call(f32[32,64,128]{2,1,0:T(8,128)S(1)} %bitcast.22, f32[8,512]{1,0:T(8,128)S(1)} %copy-done.1, f32[8,512]{1,0:T(8,128)S(1)} %copy-done.2, s32[16,512]{1,0:T(8,128)S(1)} %bitcast.25, f32[1,512]{1,0:T(1,128)S(1)} %bitcast.28, ...), custom_call_target="tpu_custom_call" | custom-call | tf_op jit(solution)/shard_map/gather/pallas_call | solution.py:356
  85.4 0.2 reduce_sum.18
  85.6 0.2 broadcast_subtract_fusion
  85.8 2.7 %fusion.18 = f32[768,512]{1,0:T(8,128)S(1)} fusion(f32[1024,768]{1,0:T(8,128)S(1)} %broadcast_subtract_fusion), kind=kOutput, calls=%fused_computation.19 | convolution fusion | flops 2416312320 | bytes 6815744 | tf_op jit(solution)/shard_map/dot_general | solution.py:466
  88.5 0.3 abs_reduce_fusion
  88.8 0.1 slice_multiply_fusion
  88.9 0.2 multiply_subtract_fusion
  89.1 1.5 fusion.6
  90.6 0.1 slice_add_fusion.4
  90.7 0.1 slice.49
  90.8 1.5 fusion.10
  92.3 0.1 slice_add_fusion.3
  92.3 0.1 slice.51
  92.4 1.5 fusion.14
  93.9 0.7 fusion.24
  94.6 1.1 fusion.21
  95.7 67.9 %scatter.1 = f32[16,64,256]{2,1,0:T(8,128)S(1)} custom-call(f32[16,64,256]{2,1,0:T(8,128)S(1)} %bitcast.24), custom_call_target="tpu_custom_call" | custom-call | tf_op jit(solution)/shard_map/scatter/pallas_call | solution.py:442
  163.6 1.6 copy.13
  (6 shorter events, 0.0 us)
Async XLA Ops:
  0.0 2.8 %copy-start.4 = (f32[1,1,512]{2,1,0:T(1,128)S(1)}, f32[1,1,512]{2,1,0:T(1,128)}, u32[]{:S(2)}) copy-start(f32[1,1,512]{2,1,0:T(1,128)} %param.13) | copy-start | bytes 6148
  0.0 2.8 %copy-start.3 = (f32[1,1,512]{2,1,0:T(1,128)S(1)}, f32[1,1,512]{2,1,0:T(1,128)}, u32[]{:S(2)}) copy-start(f32[1,1,512]{2,1,0:T(1,128)} %param.12) | copy-start | bytes 6148
  0.0 2.8 %copy-start = (s32[1,16,512]{2,1,0:T(8,128)S(1)}, s32[1,16,512]{2,1,0:T(8,128)}, u32[]{:S(2)}) copy-start(s32[1,16,512]{2,1,0:T(8,128)} %param.11) | copy-start | bytes 98308
  0.0 2.8 %copy-start.2 = (f32[8,512]{1,0:T(8,128)S(1)}, f32[8,512]{1,0:T(8,128)}, u32[]{:S(2)}) copy-start(f32[8,512]{1,0:T(8,128)} %north_wind.1) | copy-start | bytes 49156
  0.0 2.8 %copy-start.1 = (f32[8,512]{1,0:T(8,128)S(1)}, f32[8,512]{1,0:T(8,128)}, u32[]{:S(2)}) copy-start(f32[8,512]{1,0:T(8,128)} %diffusivity.1) | copy-start | bytes 49156
